TPU v7x, 32 devices: a whole 2x2x4 slice. The times are simulated.
32 devices in a mesh: gx: 8 (over z, x), gy: 4 (over y, core).
Axes of the slice: x: 2, y: 2, z: 4, core: 2. Of those that a mesh axis runs over, the one named last changes fastest.
Arguments:
- pressure: float32 [10, 64, 512], P(None, 'gx', 'gy'), may hold values from -3 to 1
- saturation_old: float32 [10, 64, 512], P(None, 'gx', 'gy'), may hold values from 0.3 to 1
- soil_type: int32 [10, 64, 512], P(None, 'gx', 'gy'), may hold values from 0 to 23
- recharge: float32 [64, 512], P('gx', 'gy'), may hold values from -6 to 6
- ksat_table: float32 [24], replicated, may hold values from 0.05 to 5
- alpha_table: float32 [24], replicated, may hold values from 0.3 to 3
- porosity_table: float32 [24], replicated, may hold values from 0.1 to 0.5
- residual_table: float32 [24], replicated, may hold values from 0.02 to 0.3
Outputs:
- pressure_new: float32 [10, 64, 512], P(None, 'gx', 'gy')
All inputs are finite; a program needn't handle non-finite values.
Results may differ from a plain program's by a relative error of at most 0.0003.
Values sent between devices are 32-bit elements; how exact they have to be, the bound alone decides.
A program may use at most 64 MiB of HBM per device.

v0:
```python
import jax
import jax.numpy as jnp
from jax import lax
from jax.sharding import PartitionSpec as P

NEWTON = 2
KRYLOV = 2
SWEEPS = 2
COARSE_SWEEPS = 4


OMEGA = 0.8
STORAGE = 0.05
EPSILON = 1e-06


def padded_2(cells, sides, width):
    for axis, dim in sides:
        count = lax.axis_size(axis)
        ends = count - 1
        head = lax.slice_in_dim(cells, 0, width, axis=dim)
        tail = lax.slice_in_dim(cells, cells.shape[dim] - width, cells.shape[dim], axis=dim)
        cells = jnp.concatenate(
            [
                lax.ppermute(tail, axis, [(i, (i + 1) % count) for i in range(ends)]),
                cells,
                lax.ppermute(head, axis, [((i + 1) % count, i) for i in range(ends)]),
            ],
            axis=dim,
        )
    return cells


def harmonic(first, second):
    return 2.0 * first * second / (first + second)


def vertical(field):
    zeros_layer = jnp.zeros_like(field[:1])
    return (
        jnp.concatenate([zeros_layer, field[:-1]], 0),
        jnp.concatenate([field[1:], zeros_layer], 0),
    )


def neighbours(padded):
    return (padded[:, :-2, 1:-1], padded[:, 2:, 1:-1], padded[:, 1:-1, :-2], padded[:, 1:-1, 2:])


def fine_padding(field):
    return padded_2(field, (("gx", 1), ("gy", 2)), 1)


def middle_padding(field):
    return padded_2(field, (("gx", 1), ("gy", 2)), 1)


def strip_padding(field):
    return jnp.pad(field, ((0, 0), (1, 1), (1, 1)))


def apply_level(field, padded, coefs):
    storage_term, west_face, east_face, south_face, north_face, lower_face, upper_face = coefs
    west, east, south, north = neighbours(padded)
    below, above = vertical(field)
    return (
        storage_term * field
        + west_face * (field - west)
        + east_face * (field - east)
        + south_face * (field - south)
        + north_face * (field - north)
        + lower_face * (field - below)
        + upper_face * (field - above)
    )


def diagonal_of(coefs):
    storage_term, west_face, east_face, south_face, north_face, lower_face, upper_face = coefs
    return storage_term + west_face + east_face + south_face + north_face + lower_face + upper_face


def blocks(field):
    depth, across, along = field.shape
    return field.reshape(depth, across // 2, 2, along // 2, 2)


def restrict(field):
    parts = blocks(field)
    return parts[:, :, 0, :, 0] + parts[:, :, 0, :, 1] + parts[:, :, 1, :, 0] + parts[:, :, 1, :, 1]


def prolong(field):
    return jnp.repeat(jnp.repeat(field, 2, axis=1), 2, axis=2)


def coarsen(coefs):
    storage_term, west_face, east_face, south_face, north_face, lower_face, upper_face = coefs
    west_parts = blocks(west_face)
    east_parts = blocks(east_face)
    south_parts = blocks(south_face)
    north_parts = blocks(north_face)
    return (
        restrict(storage_term),
        west_parts[:, :, 0, :, 0] + west_parts[:, :, 0, :, 1],
        east_parts[:, :, 1, :, 0] + east_parts[:, :, 1, :, 1],
        south_parts[:, :, 0, :, 0] + south_parts[:, :, 1, :, 0],
        north_parts[:, :, 0, :, 1] + north_parts[:, :, 1, :, 1],
        restrict(lower_face),
        restrict(upper_face),
    )


def relax(rhs, coefs, diag, rim):
    field = OMEGA * rhs / diag
    field = field + OMEGA * (rhs - apply_level(field, rim(field), coefs)) / diag
    return field


def resume(field, rhs, coefs, diag, sweeps, rim):
    for sweep in range(sweeps):
        field = field + OMEGA * (rhs - apply_level(field, rim(field), coefs)) / diag
    return field


def vcycle(rhs_fine, level_fine, level_middle, coarse_solve):
    coefs_fine, diag_fine, rim_fine = level_fine
    coefs_middle, diag_middle, rim_middle = level_middle
    fine_iter = relax(rhs_fine, coefs_fine, diag_fine, rim_fine)
    fine_resid = rhs_fine - apply_level(fine_iter, rim_fine(fine_iter), coefs_fine)
    rhs_middle = restrict(fine_resid)
    middle_iter = relax(rhs_middle, coefs_middle, diag_middle, rim_middle)
    middle_resid = rhs_middle - apply_level(middle_iter, rim_middle(middle_iter), coefs_middle)
    correction = coarse_solve(restrict(middle_resid))
    middle_iter = resume(
        middle_iter + prolong(correction), rhs_middle, coefs_middle, diag_middle, SWEEPS, rim_middle
    )
    fine_iter = resume(
        fine_iter + prolong(middle_iter), rhs_fine, coefs_fine, diag_fine, SWEEPS, rim_fine
    )
    return fine_iter


def face_terms(relative, conduct, relative_pad, conduct_pad):
    rel_west, rel_east, rel_south, rel_north = neighbours(relative_pad)
    con_west, con_east, con_south, con_north = neighbours(conduct_pad)
    rel_below, rel_above = vertical(relative)
    con_below, con_above = vertical(conduct)
    return (
        harmonic(conduct, con_west) * (0.5 * (relative + rel_west)),
        harmonic(conduct, con_east) * (0.5 * (relative + rel_east)),
        harmonic(conduct, con_south) * (0.5 * (relative + rel_south)),
        harmonic(conduct, con_north) * (0.5 * (relative + rel_north)),
        harmonic(conduct, con_below) * (0.5 * (relative + rel_below)),
        harmonic(conduct, con_above) * (0.5 * (relative + rel_above)),
    )


def flux_of(state, state_pad, faces):
    west_face, east_face, south_face, north_face, lower_face, upper_face = faces
    west, east, south, north = neighbours(state_pad)
    below, above = vertical(state)
    return (
        west_face * (state - west)
        + east_face * (state - east)
        + south_face * (state - south)
        + north_face * (state - north)
        + lower_face * (state - below + 1.0)
        + upper_face * (state - above - 1.0)
    )


def least_squares(hessen, beta, count):
    gram = [
        [
            sum((hessen[row][first] * hessen[row][second] for row in range(count + 1)))
            for second in range(count)
        ]
        for first in range(count)
    ]
    rhs = [beta * hessen[0][col] for col in range(count)]
    for pivot in range(count):
        for row in range(pivot + 1, count):
            factor = gram[row][pivot] / gram[pivot][pivot]
            for col in range(pivot, count):
                gram[row][col] = gram[row][col] - factor * gram[pivot][col]
            rhs[row] = rhs[row] - factor * rhs[pivot]
    weights = [0.0] * count
    for row in reversed(range(count)):
        total = rhs[row]
        for col in range(row + 1, count):
            total = total - gram[row][col] * weights[col]
        weights[row] = total / gram[row][row]
    return weights


def lookup(soil_type, tables):
    kinds = jnp.arange(tables.shape[1], dtype=jnp.int32)

    def layer(kinds_here):
        flat = kinds_here.reshape(-1)
        onehot = (kinds[:, None] == flat[None, :]).astype(jnp.float32)
        values = jnp.dot(
            tables, onehot, precision=lax.Precision.HIGHEST, preferred_element_type=jnp.float32
        )
        return values.reshape((tables.shape[0],) + kinds_here.shape)

    values = lax.map(layer, soil_type)
    return (values[:, 0], values[:, 1], values[:, 2], values[:, 3])


def on_device(
    pressure,
    saturation_old,
    soil_type,
    recharge,
    ksat_table,
    alpha_table,
    porosity_table,
    residual_table,
):
    tables = jnp.stack([ksat_table, alpha_table, porosity_table, residual_table])
    conduct, alpha, porosity, resid = lookup(soil_type, tables)
    top_layer = lax.broadcasted_iota(jnp.int32, pressure.shape, 0) == pressure.shape[0] - 1
    state = pressure
    for newton_step in range(NEWTON):
        effective = jax.nn.sigmoid(alpha * state)
        saturation = resid + (1.0 - resid) * effective
        slope = (1.0 - resid) * alpha * effective * (1.0 - effective)
        relative = effective * effective
        stacked = jnp.stack([state, relative, conduct])
        padded_all = padded_2(stacked, (("gx", 2), ("gy", 3)), 1)
        faces = face_terms(relative, conduct, padded_all[1], padded_all[2])
        nonlinear = (
            porosity * (saturation - saturation_old)
            + STORAGE * (state - pressure)
            + flux_of(state, padded_all[0], faces)
        )
        nonlinear = nonlinear - jnp.where(top_layer, recharge[None], 0.0)
        coefs_fine = (STORAGE + porosity * slope,) + faces
        coefs_middle = coarsen(coefs_fine)
        coefs_coarse = coarsen(coefs_middle)
        level_fine = (coefs_fine, diagonal_of(coefs_fine), fine_padding)
        level_middle = (coefs_middle, diagonal_of(coefs_middle), middle_padding)
        gathered = tuple(
            (
                lax.all_gather(coefs_coarse[0], "gy", axis=2, tiled=True),
                lax.all_gather(coefs_coarse[1], "gy", axis=2, tiled=True),
                lax.all_gather(coefs_coarse[2], "gy", axis=2, tiled=True),
                lax.all_gather(coefs_coarse[3], "gy", axis=2, tiled=True),
                lax.all_gather(coefs_coarse[4], "gy", axis=2, tiled=True),
                lax.all_gather(coefs_coarse[5], "gy", axis=2, tiled=True),
                lax.all_gather(coefs_coarse[6], "gy", axis=2, tiled=True),
            )
        )
        gathered_diag = diagonal_of(gathered)
        storage_total = jnp.sum(gathered[0], axis=(1, 2))

        def coarse_solve(rhs_coarse):
            whole = lax.all_gather(rhs_coarse, "gy", axis=2, tiled=True)
            level_mean = jnp.sum(whole, axis=(1, 2)) / storage_total
            start = jnp.zeros_like(whole) + level_mean[:, None, None]
            solved = resume(start, whole, gathered, gathered_diag, COARSE_SWEEPS, strip_padding)
            span = rhs_coarse.shape[2]
            return lax.dynamic_slice_in_dim(solved, lax.axis_index("gy") * span, span, 2)

        beta = jnp.sqrt(lax.psum(jnp.sum(nonlinear * nonlinear), ("gx", "gy")) + EPSILON)
        basis = [-nonlinear / beta]
        directions = []
        hessen = [[0.0] * KRYLOV for row in range(KRYLOV + 1)]
        for inner in range(KRYLOV):
            direction = vcycle(basis[inner], level_fine, level_middle, coarse_solve)
            directions.append(direction)
            image = apply_level(direction, fine_padding(direction), coefs_fine)
            for index in range(len(basis)):
                product = lax.psum(jnp.sum(basis[index] * image), ("gx", "gy"))
                hessen[index][inner] = product
                image = image - product * basis[index]
            norm_next = jnp.sqrt(lax.psum(jnp.sum(image * image), ("gx", "gy")) + EPSILON)
            hessen[inner + 1][inner] = norm_next
            basis.append(image / norm_next)
        weights = least_squares(hessen, beta, KRYLOV)
        for inner in range(KRYLOV):
            state = state + weights[inner] * directions[inner]
    return state


def solution(mesh):
    placed = (
        P(None, "gx", "gy"),
        P(None, "gx", "gy"),
        P(None, "gx", "gy"),
        P("gx", "gy"),
        P(),
        P(),
        P(),
        P(),
    )
    return jax.shard_map(
        on_device, mesh=mesh, in_specs=placed, out_specs=P(None, "gx", "gy"), check_vma=False
    )
```

profile of v0, /device:TPU:0, one launch (start us, length us, event | category | flops | bytes accessed | tf_op | source)
XLA Modules:
  0.0 1299.8 jit_solution(12673700631314723222)
XLA Ops:
  0.7 8.7 while.11
  12.1 5.5 collective-permute-start
  22.0 4.3 collective-permute-done.3
  28.9 44.5 %psum.84 = f32[]{:T(128)} all-reduce(f32[]{:T(128)} %get-tuple-element.97), channel_id=1, replica_groups=mesh['gx'=8,'gy'=4] {'gx','gy'}, use_global_device_ids=true, to_apply=%region_3.4 | all-reduce | flops 1 | bytes 8 | tf_op jit(solution)/shard_map/psum | solution.py:266
  76.9 4.2 collective-permute-start.4
  96.3 4.5 collective-permute-start.8
  118.0 4.7 collective-permute-start.12
  124.0 6.9 all-gather.1
  131.2 5.4 all-gather.2
  136.7 5.4 all-gather.3
  142.2 5.4 all-gather.4
  147.6 5.4 all-gather.5
  153.0 5.4 all-gather.6
  165.4 4.5 collective-permute-start.16
  171.2 6.5 all-gather.7
  185.0 6.8 all-gather
  193.1 4.5 collective-permute-start.20
  210.2 4.8 collective-permute-start.24
  233.5 4.2 collective-permute-done.29
  245.2 4.7 collective-permute-start.32
  251.3 4.2 collective-permute-done.33
  267.5 4.2 collective-permute-done.37
  280.2 40.3 %psum.85 = f32[]{:T(128)} all-reduce(f32[]{:T(128)} %get-tuple-element.85), channel_id=1, replica_groups=mesh['gx'=8,'gy'=4] {'gx','gy'}, use_global_device_ids=true, to_apply=%region_7.8 | all-reduce | flops 1 | bytes 8 | tf_op jit(solution)/shard_map/psum | solution.py:275
  321.7 41.1 %psum.86 = f32[]{:T(128)} all-reduce(f32[]{:T(128)} %multiply_reduce_fusion.9), channel_id=1, replica_groups=mesh['gx'=8,'gy'=4] {'gx','gy'}, use_global_device_ids=true, to_apply=%region_9.10 | all-reduce | flops 1 | bytes 8 | tf_op jit(solution)/shard_map/psum | solution.py:278
  364.2 4.2 collective-permute-start.40
  369.7 4.2 collective-permute-done.41
  385.0 4.2 collective-permute-done.45
  432.9 6.8 all-gather.8
  456.7 4.6 collective-permute-start.60
  480.6 4.2 collective-permute-done.65
  496.5 4.2 collective-permute-done.69
  525.4 39.4 %psum.87 = f32[]{:T(128)} all-reduce(f32[]{:T(128)} %get-tuple-element.79), channel_id=1, replica_groups=mesh['gx'=8,'gy'=4] {'gx','gy'}, use_global_device_ids=true, to_apply=%region_12.13 | all-reduce | flops 1 | bytes 8 | tf_op jit(solution)/shard_map/psum | solution.py:275
  568.9 42.2 %psum.88 = f32[]{:T(128)} all-reduce(f32[]{:T(128)} %multiply_reduce_fusion.7), channel_id=1, replica_groups=mesh['gx'=8,'gy'=4] {'gx','gy'}, use_global_device_ids=true, to_apply=%region_14.15 | all-reduce | flops 1 | bytes 8 | tf_op jit(solution)/shard_map/psum | solution.py:275
  614.2 39.2 %psum.89 = f32[]{:T(128)} all-reduce(f32[]{:T(128)} %multiply_reduce_fusion.6), channel_id=1, replica_groups=mesh['gx'=8,'gy'=4] {'gx','gy'}, use_global_device_ids=true, to_apply=%region_16.17 | all-reduce | flops 1 | bytes 8 | tf_op jit(solution)/shard_map/psum | solution.py:278
  655.8 4.2 collective-permute-start.76
  675.2 43.7 %psum.90 = f32[]{:T(128)} all-reduce(f32[]{:T(128)} %get-tuple-element.68), channel_id=1, replica_groups=mesh['gx'=8,'gy'=4] {'gx','gy'}, use_global_device_ids=true, to_apply=%region_18.19 | all-reduce | flops 1 | bytes 8 | tf_op jit(solution)/shard_map/psum | solution.py:266
  738.2 5.2 collective-permute-start.84
  745.1 4.8 collective-permute-done.85
  761.0 7.2 all-gather.10
  769.1 4.8 collective-permute-start.88
  775.2 5.4 all-gather.11
  780.7 5.4 all-gather.12
  786.2 5.4 all-gather.13
  791.7 5.4 all-gather.14
  797.1 5.4 all-gather.15
  809.3 4.5 collective-permute-start.92
  815.1 6.5 all-gather.16
  828.9 6.8 all-gather.9
  837.1 4.5 collective-permute-start.96
  854.2 4.6 collective-permute-start.100
  877.2 4.2 collective-permute-done.105
  894.3 4.2 collective-permute-done.109
  910.5 4.2 collective-permute-done.113
  923.2 40.5 %psum.91 = f32[]{:T(128)} all-reduce(f32[]{:T(128)} %get-tuple-element.55), channel_id=1, replica_groups=mesh['gx'=8,'gy'=4] {'gx','gy'}, use_global_device_ids=true, to_apply=%region_22.23 | all-reduce | flops 1 | bytes 8 | tf_op jit(solution)/shard_map/psum | solution.py:275
  965.0 41.1 %psum.92 = f32[]{:T(128)} all-reduce(f32[]{:T(128)} %multiply_reduce_fusion.3), channel_id=1, replica_groups=mesh['gx'=8,'gy'=4] {'gx','gy'}, use_global_device_ids=true, to_apply=%region_24.25 | all-reduce | flops 1 | bytes 8 | tf_op jit(solution)/shard_map/psum | solution.py:278
  1013.0 4.2 collective-permute-done.117
  1028.4 4.2 collective-permute-done.121
  1076.2 6.8 all-gather.17
  1100.2 4.5 collective-permute-start.136
  1124.1 4.2 collective-permute-done.141
  1140.0 4.2 collective-permute-done.145
  1168.9 39.3 %psum.93 = f32[]{:T(128)} all-reduce(f32[]{:T(128)} %get-tuple-element.51), channel_id=1, replica_groups=mesh['gx'=8,'gy'=4] {'gx','gy'}, use_global_device_ids=true, to_apply=%region_27.28 | all-reduce | flops 1 | bytes 8 | tf_op jit(solution)/shard_map/psum | solution.py:275
  1212.8 42.2 %psum.94 = f32[]{:T(128)} all-reduce(f32[]{:T(128)} %multiply_reduce_fusion.1), channel_id=1, replica_groups=mesh['gx'=8,'gy'=4] {'gx','gy'}, use_global_device_ids=true, to_apply=%region_29.30 | all-reduce | flops 1 | bytes 8 | tf_op jit(solution)/shard_map/psum | solution.py:275
  1258.2 39.1 %psum.95 = f32[]{:T(128)} all-reduce(f32[]{:T(128)} %multiply_reduce_fusion), channel_id=1, replica_groups=mesh['gx'=8,'gy'=4] {'gx','gy'}, use_global_device_ids=true, to_apply=%region_31.32 | all-reduce | flops 1 | bytes 8 | tf_op jit(solution)/shard_map/psum | solution.py:278
  (874 shorter events, 529.1 us)
Async XLA Ops:
  10.8 8.3 collective-permute-start.1
  12.1 6.9 collective-permute-start
  20.6 5.6 collective-permute-start.3
  76.9 12.2 collective-permute-start.4
  81.1 8.0 collective-permute-start.5
  90.7 5.5 collective-permute-start.7
  96.3 6.1 collective-permute-start.8
  100.9 5.5 collective-permute-start.9
  118.0 40.4 %collective-permute-start.12 = (f32[10,1,64]{0,2,1:T(8,128)S(1)}, f32[10,1,64]{0,2,1:T(8,128)S(1)}, u32[]{:S(2)}, u32[]{:S(2)}) collective-permute-start(f32[10,1,64]{0,2,1:T(8,128)S(1)} %get-tuple-element.229), channel_id=1, source_target_pairs={{0,4},{4,8},{8,12},{12,16},{16,20},{20,24},{24,28},{1,5},{5,9},{9,... | collective-permute-start | bytes 7688 | tf_op jit(solution)/shard_map/ppermute | solution.py:25
  122.7 35.8 %collective-permute-start.13 = (f32[10,1,64]{0,2,1:T(8,128)S(1)}, f32[10,1,64]{0,2,1:T(8,128)S(1)}, u32[]{:S(2)}, u32[]{:S(2)}) collective-permute-start(f32[10,1,64]{0,2,1:T(8,128)S(1)} %get-tuple-element.230), channel_id=1, source_target_pairs={{4,0},{8,4},{12,8},{16,12},{20,16},{24,20},{28,24},{5,1},{9,5},{13... | collective-permute-start | bytes 7688 | tf_op jit(solution)/shard_map/ppermute | solution.py:27
  165.4 12.6 collective-permute-start.16
  169.9 8.1 collective-permute-start.17
  193.1 6.1 collective-permute-start.20
  197.7 5.8 collective-permute-start.21
  210.2 6.4 collective-permute-start.24
  215.0 5.8 collective-permute-start.25
  232.2 5.5 collective-permute-start.29
  245.2 6.1 collective-permute-start.32
  250.0 5.5 collective-permute-start.33
  266.2 5.5 collective-permute-start.37
  364.2 5.5 collective-permute-start.40
  368.4 5.5 collective-permute-start.41
  375.3 5.4 collective-permute-start.43
  383.7 5.5 collective-permute-start.45
  401.1 5.8 collective-permute-start.49
  419.0 5.8 collective-permute-start.53
  444.2 5.8 collective-permute-start.57
  456.7 6.1 collective-permute-start.60
  461.3 5.8 collective-permute-start.61
  479.3 5.5 collective-permute-start.65
  495.2 5.5 collective-permute-start.69
  508.6 6.1 collective-permute-start.72
  511.4 5.5 collective-permute-start.73
  655.8 5.6 collective-permute-start.76
  660.0 5.6 collective-permute-start.77
  721.6 11.2 collective-permute-start.80
  725.8 7.1 collective-permute-start.81
  738.2 6.8 collective-permute-start.84
  743.5 6.4 collective-permute-start.85
  750.0 5.4 collective-permute-start.86
  769.1 33.4 %collective-permute-start.88 = (f32[10,1,64]{0,2,1:T(8,128)S(1)}, f32[10,1,64]{0,2,1:T(8,128)S(1)}, u32[]{:S(2)}, u32[]{:S(2)}) collective-permute-start(f32[10,1,64]{0,2,1:T(8,128)S(1)} %get-tuple-element.197), channel_id=1, source_target_pairs={{0,4},{4,8},{8,12},{12,16},{16,20},{20,24},{24,28},{1,5},{5,9},{9,... | collective-permute-start | bytes 7688 | tf_op jit(solution)/shard_map/ppermute | solution.py:25
  773.9 28.6 %collective-permute-start.89 = (f32[10,1,64]{0,2,1:T(8,128)S(1)}, f32[10,1,64]{0,2,1:T(8,128)S(1)}, u32[]{:S(2)}, u32[]{:S(2)}) collective-permute-start(f32[10,1,64]{0,2,1:T(8,128)S(1)} %get-tuple-element.198), channel_id=1, source_target_pairs={{4,0},{8,4},{12,8},{16,12},{20,16},{24,20},{28,24},{5,1},{9,5},{13... | collective-permute-start | bytes 7688 | tf_op jit(solution)/shard_map/ppermute | solution.py:27
  809.3 12.6 collective-permute-start.92
  813.8 8.1 collective-permute-start.93
  837.1 6.1 collective-permute-start.96
  841.6 5.8 collective-permute-start.97
  854.2 6.2 collective-permute-start.100
  858.8 5.8 collective-permute-start.101
  875.9 5.5 collective-permute-start.105
  893.0 5.5 collective-permute-start.109
  909.2 5.5 collective-permute-start.113
  1007.5 5.5 collective-permute-start.116
  1011.7 5.5 collective-permute-start.117
  1018.6 5.5 collective-permute-start.119
  1027.1 5.5 collective-permute-start.121
  1044.6 5.8 collective-permute-start.125
  1062.3 5.8 collective-permute-start.129
  1087.7 5.8 collective-permute-start.133
  1100.2 6.1 collective-permute-start.136
  1104.7 5.8 collective-permute-start.137
  1122.8 5.5 collective-permute-start.141
  1138.7 5.5 collective-permute-start.145
  1152.1 6.1 collective-permute-start.148
  1154.9 5.5 collective-permute-start.149
  (122 other events, 420.2 us)
where the time goes:
time: 1310 us; the launch traced here: 1300 us
  blocking collectives  601 us (46%)
  starting transfers between devices  350 us (27%)
  waiting for transfers between devices  238 us (18%)
  local copies, waits for them, and re-layouts  50.8 us (4%)
  other arithmetic  34.8 us (3%)
  between operations  22.8 us (2%)
    ppermute x76, starting transfers between devices, padded_2(): lax.ppermute(tail, axis, [(i, (i + 1) % count) for i in range(ends)])  251 us
    psum x6, blocking collectives, on_device(): product = lax.psum(jnp.sum(basis[index] * image), ('gx', 'gy'))  244 us
    ppermute x76, waiting for transfers between devices, padded_2(): lax.ppermute(head, axis, [((i + 1) % count, i) for i in range(ends)])  234 us
    psum x4, blocking collectives, on_device(): lax.psum(jnp.sum(image * image), ('gx', 'gy')) + EPSILON  161 us
    ppermute x76, starting transfers between devices, padded_2(): lax.ppermute(head, axis, [((i + 1) % count, i) for i in range(ends)])  99.3 us
    psum x2, blocking collectives, on_device(): lax.psum(jnp.sum(nonlinear * nonlinear), ('gx', 'gy')) + EPSILON  88.2 us
    all_gather x4, blocking collectives, coarse_solve(): whole = lax.all_gather(rhs_coarse, 'gy', axis=2, tiled=True)  27.3 us
  transfers between devices with their start and end apart: 152, of which 83 were waited for; matrix products, arithmetic and copies ran while one was open for 1% of the time, Pallas kernels for 0%

commit v1 on v0

v1 whole, which is shorter than its diff:
```python
import functools

import jax
import jax.numpy as jnp
from jax import lax
from jax.experimental import pallas as pl
from jax.experimental.pallas import tpu as pltpu
from jax.sharding import PartitionSpec as P

NEWTON = 2
COARSE_SWEEPS = 4
OMEGA = 0.8
STORAGE = 0.05
EPSILON = 1e-06

ROWS = 24
LANES = 256
TILE = (8, 128)
MESH = pl.DeviceIdType.MESH
DIRECTIONS = tuple((dx, dy) for dx in (-1, 0, 1) for dy in (-1, 0, 1) if (dx, dy) != (0, 0))
HALO = 3


def roll(field, shift, axis):
    size = field.shape[axis]
    return pltpu.roll(field, shift % size if isinstance(shift, int) else shift, axis)


def iota(shape, axis):
    return lax.broadcasted_iota(jnp.int32, shape, axis)


def pair(field, step, axis):
    low = (iota(field.shape, axis) & step) == 0
    return jnp.where(low, roll(field, -step, axis), roll(field, step, axis))


def sum_pair(field, step, axis):
    return field + pair(field, step, axis)


def sum_four(field, step):
    return sum_pair(sum_pair(field, step, 1), step, 0)


def spread_low(field, step, axis):
    low = (iota(field.shape, axis) & step) == 0
    return jnp.where(low, field, roll(field, step, axis))


def spread_high(field, step, axis):
    low = (iota(field.shape, axis) & step) == 0
    return jnp.where(low, roll(field, -step, axis), field)


def coarsen(coefs, step):
    storage, west, east, south, north, lower, upper = coefs
    return (
        sum_four(storage, step),
        spread_low(sum_pair(west, step, 1), step, 0),
        spread_high(sum_pair(east, step, 1), step, 0),
        spread_low(sum_pair(south, step, 0), step, 1),
        spread_high(sum_pair(north, step, 0), step, 1),
        sum_four(lower, step),
        sum_four(upper, step),
    )


def kernel(
    gxn, gyn, depth,
    pressure, saturation_old, soil_type, recharge, ksat, alpha_t, porosity_t, residual_t,
    out,
    old, state, sat, con, alp, por, res, rch, rel,
    lev0, lev1, g, b0, xa, xb, b1, ya, yb, z0,
    own, msg0, recv0_w, recv0_e, pack0, recv0_n, recv0_s,
    msg, recv_w, recv_e, pack, recv_n, recv_s,
    msgz, recvz_w, recvz_e, packz, recvz_n, recvz_s,
    coarse_out, coarse_in, rhs_out, rhs_in, strip, strip_sum, solved,
    part_out, part_y, part_x, whole_x,
    s0, r0, sh, rh, sz, rz, sc, rc, sb, rb, sy, ry, sx, rx,
):
    gx, gy = lax.axis_index("gx"), lax.axis_index("gy")
    has_w, has_e = gx > 0, gx < gxn - 1
    has_s, has_n = gy > 0, gy < gyn - 1
    last = depth - 1

    def inside(dx, dy):
        x, y = gx + dx, gy + dy
        return (x >= 0) & (x < gxn) & (y >= 0) & (y < gyn)

    def place(dx, dy):
        return (jnp.clip(gx + dx, 0, gxn - 1), jnp.clip(gy + dy, 0, gyn - 1))

    for ref in (recv0_w, recv0_e, recv0_n, recv0_s, recv_w, recv_e, recv_n, recv_s,
                recvz_w, recvz_e, recvz_n, recvz_s, coarse_in, rhs_in, pack0, pack, packz):
        ref[...] = jnp.zeros(ref.shape, ref.dtype)

    barrier = pltpu.get_barrier_semaphore()
    for dx in (-1, 0, 1):
        for j in range(gyn):
            if (dx, j) != (0, 0):
                @pl.when(inside(dx, 0))
                def _():
                    pl.semaphore_signal(barrier, inc=1, device_id=(jnp.clip(gx + dx, 0, gxn - 1), lax.rem(gy + j, gyn)), device_id_type=MESH)
    for j in range(1, gxn):
        x = lax.rem(gx + j, gxn)
        @pl.when((x != gx - 1) & (x != gx + 1))
        def _():
            pl.semaphore_signal(barrier, inc=1, device_id=(x, gy), device_id_type=MESH)
    strips = 1 + has_w.astype(jnp.int32) + has_e.astype(jnp.int32)
    pl.semaphore_wait(barrier, gyn * strips - 1 + gxn - strips)

    lane8, row8 = iota(TILE, 1), iota(TILE, 0)
    slot8 = (row8 & 3) * 4 + (lane8 & 3)
    lane_e, row_e = iota((ROWS, LANES), 1), iota((ROWS, LANES), 0)
    lane24 = iota((ROWS, 128), 1)
    even_row = (row_e & 1) == 0

    def put_edges(packs, k, block):
        at = lax.rem(k, 16)
        moved = roll(block, at * 8, 1)
        group = lane8 >> 3
        where = k // 16
        packs[0, where] = jnp.where(group == at, moved, packs[0, where])
        packs[1, where] = jnp.where(group == lax.rem(at + 15, 16), moved, packs[1, where])

    def halo_copies(blocks, packs, to_w, to_e, to_n, to_s, send, recv):
        copies = []
        for d, (dx, dy) in enumerate(DIRECTIONS):
            rows = pl.ds(8 * (1 - dx), 8)
            if dy == 0:
                src, dst = blocks, (to_w if dx > 0 else to_e)
            elif dy > 0:
                src, dst = packs.at[1], to_s.at[:, rows]
            else:
                src, dst = packs.at[0], to_n.at[:, rows]
            copy = pltpu.make_async_remote_copy(
                src_ref=src, dst_ref=dst, send_sem=send.at[d], recv_sem=recv.at[d],
                device_id=place(dx, dy), device_id_type=MESH)
            copies.append((copy, inside(dx, dy), inside(-dx, -dy)))
        return copies

    def gather_copies(src, dst, send, recv):
        copies = []
        for dx in (-1, 0, 1):
            for j in range(gyn):
                if (dx, j) == (0, 0):
                    continue
                copy = pltpu.make_async_remote_copy(
                    src_ref=src, dst_ref=dst.at[1 - dx, gy], send_sem=send.at[1 - dx, j], recv_sem=recv.at[1 - dx, j],
                    device_id=(jnp.clip(gx + dx, 0, gxn - 1), lax.rem(gy + j, gyn)), device_id_type=MESH)
                copies.append((copy, inside(dx, 0), inside(-dx, 0)))
        return copies

    def sum_copies(src, dst, send, recv, count, along_x):
        copies = []
        for j in range(1, count):
            to = (lax.rem(gx + j, gxn), gy) if along_x else (gx, lax.rem(gy + j, gyn))
            copy = pltpu.make_async_remote_copy(
                src_ref=src, dst_ref=dst.at[j], send_sem=send.at[j], recv_sem=recv.at[j],
                device_id=to, device_id_type=MESH)
            copies.append((copy, None, None))
        return copies

    def each(copies, do, which):
        for entry in copies:
            if entry[which] is None:
                do(entry[0])
            else:
                @pl.when(entry[which])
                def _():
                    do(entry[0])

    def start(copies):
        each(copies, lambda copy: copy.start(), 1)

    def arrive(copies):
        each(copies, lambda copy: copy.wait_recv(), 2)

    def sent(copies):
        each(copies, lambda copy: copy.wait_send(), 1)

    def extended(k, block, from_w, from_e, from_n, from_s):
        left = jnp.concatenate([from_w[k], block, from_e[k]], axis=0)
        back = lax.rem(16 - lax.rem(k, 16), 16) * 8
        where = k // 16
        north, south = roll(from_n[where], back, 1), roll(from_s[where], back, 1)
        right = jnp.where(lane24 < 8, north, jnp.where(lane24 >= 120, south, 0.0))
        return jnp.concatenate([left, right], axis=1)

    def layers(body, count=depth):
        def step(k, carry):
            body(k)
            return carry
        lax.fori_loop(0, count, step, 0)

    def stage(k):
        msg0[k] = pressure[k]
        msg0[depth + k] = saturation_old[k]
        msg0[2 * depth + k] = soil_type[k].astype(jnp.float32)
    layers(stage)
    msg0[3 * depth] = recharge[...]
    layers(lambda k: put_edges(pack0, k, msg0[k]), 3 * depth + 1)
    first = halo_copies(msg0, pack0, recv0_w, recv0_e, recv0_n, recv0_s, s0, r0)
    start(first)
    arrive(first)

    valid = (
        ((row_e >= 8) | has_w) & ((row_e < 16) | has_e)
        & ((lane_e < 128) | ((lane_e < 136) & has_n) | ((lane_e >= 248) & has_s))
    )

    def first_ext(k):
        return extended(k, msg0[k], recv0_w, recv0_e, recv0_n, recv0_s)

    def unpack_inputs(k):
        old[k] = first_ext(k)
        state[k] = old[k]
        sat[k] = first_ext(depth + k)
        soil = first_ext(2 * depth + k)
        values = [jnp.zeros((ROWS, LANES), jnp.float32) for _ in range(4)]
        for kind in range(ksat.shape[0]):
            here = soil == float(kind)
            values = [jnp.where(here, table[kind], value) for table, value in zip((ksat, alpha_t, porosity_t, residual_t), values)]
        con[k] = jnp.where(valid, values[0], 0.0)
        alp[k], por[k], res[k] = values[1], values[2], values[3]
    layers(unpack_inputs)
    rch[...] = first_ext(3 * depth)
    sent(first)

    def pulled(level, ref, k, field, step):
        total = level[2, k] * roll(field, step, 0) + level[3, k] * roll(field, -step, 0)
        total = total + level[4, k] * roll(field, step, 1) + level[5, k] * roll(field, -step, 1)
        below, above = ref[jnp.maximum(k - 1, 0)], ref[jnp.minimum(k + 1, last)]
        return total + level[6, k] * below + level[7, k] * above

    def residual(level, ref, rhs, k, step):
        field = ref[k]
        return field, rhs[k] - level[0, k] * field + pulled(level, ref, k, field, step)

    def sweep(level, src, rhs, dst, step):
        def body(k):
            field, left = residual(level, src, rhs, k, step)
            dst[k] = field + level[1, k] * left
        layers(body)

    def precondition(nt, j, rhs, gathers, received, first_of_step):
        def begin(k):
            xa[k] = lev0[1, k] * rhs[k]
        layers(begin)
        sweep(lev0, xa, rhs, xb, 1)

        def down(k):
            _, left = residual(lev0, xb, rhs, k, 1)
            total = sum_four(left, 1)
            b1[k] = total
            ya[k] = lev1[1, k] * total
        layers(down)
        sweep(lev1, ya, b1, yb, 2)
        turn = 2 * j

        def deep(k, packed):
            field, left = residual(lev1, yb, b1, k, 2)
            total = sum_four(left[8:16, :128], 2)
            mix = jnp.where((row8 & 1) == 0, field[8:16, :128], b1[k][8:16, :128])
            msg[nt, turn, k] = mix
            put_edges(pack.at[nt, turn], k, mix)
            return jnp.where(slot8 == k, total, packed)
        packed = lax.fori_loop(0, depth, deep, jnp.zeros(TILE, jnp.float32))
        if first_of_step:
            coarse_out[nt, 7] = packed
            coarse_in[nt, 1, gy] = coarse_out[nt]
        else:
            rhs_out[nt] = packed
            rhs_in[nt, 1, gy] = packed
        halo = halo_copies(msg.at[nt, turn], pack.at[nt, turn], recv_w.at[nt, turn], recv_e.at[nt, turn],
                           recv_n.at[nt, turn], recv_s.at[nt, turn], sh.at[nt, turn], rh.at[nt, turn])
        start(gathers)
        start(halo)
        arrive(gathers)

        def strips_of(pick):
            return jnp.concatenate(
                [jnp.concatenate([pick(s, y) for y in range(gyn)], axis=1) for s in range(3)], axis=0)

        width = 128 * gyn
        wide_lane, wide_row = iota((ROWS, width), 1), iota((ROWS, width), 0)

        def strip_totals(field):
            total = field[:, :128]
            for y in range(1, gyn):
                total = total + field[:, 128 * y:128 * (y + 1)]
            for step in (4, 8, 16, 32, 64):
                total = total + roll(total, step, 1)
            return sum_pair(total, 4, 0)

        if first_of_step:
            parts = [strips_of(lambda s, y: coarse_in[nt, s, y, f]) for f in range(7)]
            diag = parts[0]
            for part in parts[1:]:
                diag = diag + part
            live = diag > 0.0
            strip[0] = diag
            strip[1] = jnp.where(live, OMEGA / jnp.where(live, diag, 1.0), 0.0)
            half = (wide_row & 4) == 0
            strip[2] = jnp.where(half, 0.0, parts[1])
            strip[3] = jnp.where(half, parts[2], 0.0)
            for f in range(3, 7):
                strip[f + 1] = parts[f]
            strip_sum[...] = strip_totals(parts[0])
            b2 = strips_of(lambda s, y: coarse_in[nt, s, y, 7])
        else:
            b2 = strips_of(lambda s, y: rhs_in[nt, s, y])
        below_sum = strip_sum[...]
        some = below_sum > 0.0
        mean = jnp.where(some, strip_totals(b2) / jnp.where(some, below_sum, 1.0), 0.0)

        def coarse_sweep(_, e):
            up1, up2 = roll(e, 1, 1), roll(roll(e, 1, 0), -3, 1)
            below = jnp.where((wide_lane & 3) == 0, up2, up1)
            dn1, dn2 = roll(e, -1, 1), roll(roll(e, -1, 0), 3, 1)
            above = jnp.where((wide_lane & 3) == 3, dn2, dn1)
            total = b2 - strip[0] * e
            total = total + strip[2] * roll(e, 4, 0) + strip[3] * roll(e, -4, 0)
            total = total + strip[4] * roll(e, 4, 1) + strip[5] * roll(e, -4, 1)
            total = total + strip[6] * below + strip[7] * above
            return e + strip[1] * total
        e2 = lax.fori_loop(0, COARSE_SWEEPS, coarse_sweep, jnp.concatenate([mean] * gyn, axis=1))
        for y in range(gyn):
            solved[y] = e2[:, 128 * y:128 * (y + 1)]
        right = jnp.where(lane24 < 64, solved[jnp.minimum(gy + 1, gyn - 1)], solved[jnp.maximum(gy - 1, 0)])
        around = jnp.concatenate([solved[gy], right], axis=1)
        slot_e = (row_e & 3) * 4 + (lane_e & 3)
        arrive(halo)

        def up(k):
            m = jnp.where(slot_e == k, around, 0.0)
            m = roll(m, lax.rem(LANES - (k & 3), LANES), 1)
            m = m + roll(m, 1, 1)
            m = m + roll(m, 2, 1)
            m = roll(m, lax.rem(ROWS - (k >> 2), ROWS), 0)
            m = m + roll(m, 1, 0)
            m = m + roll(m, 2, 0)
            mix = extended(k, msg[nt, turn, k], recv_w.at[nt, turn], recv_e.at[nt, turn],
                           recv_n.at[nt, turn], recv_s.at[nt, turn])
            ya[k] = m + jnp.where(even_row, mix, roll(mix, 1, 0))
            b1[k] = jnp.where(even_row, roll(mix, -1, 0), mix)
        layers(up)
        sweep(lev1, ya, b1, yb, 2)

        def join(k):
            field, left = residual(lev1, yb, b1, k, 2)
            xb[k] = xb[k] + field + lev1[1, k] * left
        layers(join)
        sweep(lev0, xb, rhs, xa, 1)
        sweep(lev0, xa, rhs, xb, 1)
        sent(gathers)
        sent(halo)

    def applied(k):
        field = xb[k]
        return (lev0[0, k] * field - pulled(lev0, xb, k, field, 1))[8:16, :128]

    def newton(nt, carry):
        def cells(k):
            effective = 1.0 / (1.0 + jnp.exp(-(alp[k] * state[k])))
            saturation = res[k] + (1.0 - res[k]) * effective
            slope = (1.0 - res[k]) * alp[k] * effective * (1.0 - effective)
            rel[k] = effective * effective
            xa[k] = STORAGE + por[k] * slope
            g[k] = por[k] * (saturation - sat[k]) + STORAGE * (state[k] - old[k])
        layers(cells)

        def faces(k):
            def face(con_n, rel_n):
                total = con[k] + con_n
                live = total > 0.0
                return 2.0 * con[k] * con_n / jnp.where(live, total, 1.0) * (0.5 * (rel[k] + rel_n))
            west = face(roll(con[k], 1, 0), roll(rel[k], 1, 0))
            south = face(roll(con[k], 1, 1), roll(rel[k], 1, 1))
            lower = face(con[jnp.maximum(k - 1, 0)], rel[jnp.maximum(k - 1, 0)])
            lev0[2, k], lev0[3, k] = west, roll(west, -1, 0)
            lev0[4, k], lev0[5, k] = south, roll(south, -1, 1)
            lev0[6, k] = jnp.where(k > 0, lower, 0.0)
        layers(faces)

        def operators(k):
            west, east, south, north, lower = (lev0[f, k] for f in range(2, 7))
            upper = jnp.where(k < last, lev0[6, jnp.minimum(k + 1, last)], 0.0)
            lev0[7, k] = upper
            fine = (xa[k], west, east, south, north, lower, upper)
            diag = fine[0] + west + east + south + north + lower + upper
            lev0[0, k], lev0[1, k] = diag, OMEGA / diag
            here = state[k]
            below, above = state[jnp.maximum(k - 1, 0)], state[jnp.minimum(k + 1, last)]
            flux = (
                west * (here - roll(here, 1, 0)) + east * (here - roll(here, -1, 0))
                + south * (here - roll(here, 1, 1)) + north * (here - roll(here, -1, 1))
                + lower * (here - below + 1.0) + upper * (here - above - 1.0)
            )
            g[k] = jnp.where(k == last, rch[...], 0.0) - g[k] - flux
            middle = coarsen(fine, 1)
            diag = middle[0]
            for f in range(1, 7):
                lev1[f + 1, k] = middle[f]
                diag = diag + middle[f]
            lev1[0, k], lev1[1, k] = diag, OMEGA / diag
            coarse = coarsen([field[8:16, :128] for field in middle], 2)
            for f in range(7):
                coarse_out[nt, f] = jnp.where(slot8 == k, coarse[f], coarse_out[nt, f])
        for f in range(7):
            coarse_out[nt, f] = jnp.zeros(TILE, jnp.float32)
        layers(operators)

        coarse = gather_copies(coarse_out.at[nt], coarse_in.at[nt], sc.at[nt], rc.at[nt])
        precondition(nt, 0, g, coarse, coarse_in, True)

        zeros = jnp.zeros(TILE, jnp.float32)

        def image(k, sums):
            gg, gp, pp = sums
            mine = g[k][8:16, :128]
            diff = applied(k) - mine
            z0[k] = xb[k][8:16, :128]
            msgz[nt, k] = z0[k]
            put_edges(packz.at[nt], k, z0[k])
            own[k] = diff
            msg[nt, 1, k] = diff
            put_edges(pack.at[nt, 1], k, diff)
            return gg + mine * mine, gp + mine * diff, pp + diff * diff
        gg, gp, pp = lax.fori_loop(0, depth, image, (zeros, zeros, zeros))
        halo = halo_copies(msg.at[nt, 1], pack.at[nt, 1], recv_w.at[nt, 1], recv_e.at[nt, 1],
                           recv_n.at[nt, 1], recv_s.at[nt, 1], sh.at[nt, 1], rh.at[nt, 1])
        start(halo)
        arrive(halo)

        def spread(k):
            b0[k] = extended(k, own[k], recv_w.at[nt, 1], recv_e.at[nt, 1], recv_n.at[nt, 1], recv_s.at[nt, 1])
        layers(spread)
        sent(halo)

        right_sides = gather_copies(rhs_out.at[nt], rhs_in.at[nt], sb.at[nt], rb.at[nt])
        precondition(nt, 1, b0, right_sides, rhs_in, False)

        def second(k, sums):
            gs, ps, ss = sums
            mine = g[k][8:16, :128]
            im = applied(k)
            u = xb[k][8:16, :128]
            msgz[nt, depth + k] = u
            put_edges(packz.at[nt], depth + k, u)
            return gs + mine * im, ps + own[k] * im, ss + im * im
        gs, ps, ss = lax.fori_loop(0, depth, second, (zeros, zeros, zeros))

        rows = [jnp.sum(item, axis=0, keepdims=True) for item in (gg, gp, pp, gs, ps, ss)]
        tile = zeros
        for i, item in enumerate(rows):
            tile = jnp.where(row8 == i, jnp.broadcast_to(item, TILE), tile)
        part_out[nt] = tile
        along_y = sum_copies(part_out.at[nt], part_y.at[nt], sy.at[nt], ry.at[nt], gyn, False)
        start(along_y)
        basis = halo_copies(msgz.at[nt], packz.at[nt], recvz_w.at[nt], recvz_e.at[nt],
                            recvz_n.at[nt], recvz_s.at[nt], sz.at[nt], rz.at[nt])

        @pl.when(nt < NEWTON - 1)
        def _():
            start(basis)
        arrive(along_y)
        for j in range(1, gyn):
            tile = tile + part_y[nt, j]
        whole_x[nt] = tile
        along_x = sum_copies(whole_x.at[nt], part_x.at[nt], sx.at[nt], rx.at[nt], gxn, True)
        start(along_x)
        arrive(along_x)
        for j in range(1, gxn):
            tile = tile + part_x[nt, j]
        totals = jnp.broadcast_to(jnp.sum(tile, axis=1, keepdims=True), (8, LANES))
        gg, gp, pp, gs, ps, ss = (totals[i:i + 1] for i in range(6))

        square = gg + EPSILON
        beta = jnp.sqrt(square)
        h00 = (gg + gp) / square
        a = (EPSILON - gp) / square
        vv = jnp.maximum(pp + 2.0 * a * gp + a * a * gg, 0.0)
        h10 = jnp.sqrt(vv / square + EPSILON)
        kappa = 1.0 / (beta * h10)
        gw = gs + a * gp + a * gg
        h01 = kappa / beta * gw
        h11 = kappa * kappa * (ps + a * pp + a * gp + a * gw)
        ww = kappa * kappa * (ss + 2.0 * a * (ps + gs) + a * a * (pp + 2.0 * gp + gg))
        v00 = gg / square
        v11 = kappa * kappa * vv
        v01 = kappa / beta * (gp + a * gg)
        rest = ww - h01 * h01 * (2.0 - v00) - h11 * h11 * (2.0 - v11) + 2.0 * h01 * h11 * v01
        h21_sq = jnp.maximum(rest, 0.0) + EPSILON
        m00 = h00 * h00 + h10 * h10
        m01 = h00 * h01 + h10 * h11
        m11 = h01 * h01 + h11 * h11 + h21_sq
        q0, q1 = beta * h00, beta * h01
        factor = m01 / m00
        y1 = (q1 - factor * q0) / (m11 - factor * m01)
        y0 = (q0 - m01 * y1) / m00
        first_weight = y0 / beta + y1 * kappa * a
        second_weight = y1 * kappa

        @pl.when(nt < NEWTON - 1)
        def _():
            arrive(basis)

            def advance(k):
                z = extended(k, z0[k], recvz_w.at[nt], recvz_e.at[nt], recvz_n.at[nt], recvz_s.at[nt])
                u = extended(depth + k, msgz[nt, depth + k], recvz_w.at[nt], recvz_e.at[nt], recvz_n.at[nt], recvz_s.at[nt])
                state[k] = state[k] + first_weight * z + second_weight * u
            layers(advance)
            sent(basis)

        @pl.when(nt == NEWTON - 1)
        def _():
            def finish(k):
                out[k] = (state[k][8:16, :128] + first_weight[:, :128] * z0[k]
                          + second_weight[:, :128] * msgz[nt, depth + k])
            layers(finish)
        sent(along_y)
        sent(along_x)
        return carry

    lax.fori_loop(0, NEWTON, newton, 0)


def on_device(gxn, gyn, *args):
    depth = args[0].shape[0]

    def vmem(*shape):
        return pltpu.VMEM(shape, jnp.float32)

    def dma(*shape):
        return pltpu.SemaphoreType.DMA(shape)

    ext = vmem(depth, ROWS, LANES)
    level = vmem(8, depth, ROWS, LANES)
    n0 = 3 * depth + 1
    p0 = (n0 + 15) // 16
    pz = (2 * depth + 15) // 16
    scratch = [ext] * 7 + [vmem(ROWS, LANES), ext]
    scratch += [level, level] + [ext] * 7 + [vmem(depth, *TILE)]
    scratch += [
        vmem(depth, *TILE), vmem(n0, *TILE), vmem(n0, *TILE), vmem(n0, *TILE),
        vmem(2, p0, *TILE), vmem(p0, ROWS, 128), vmem(p0, ROWS, 128),
        vmem(NEWTON, HALO, depth, *TILE), vmem(NEWTON, HALO, depth, *TILE), vmem(NEWTON, HALO, depth, *TILE),
        vmem(NEWTON, HALO, 2, 1, *TILE), vmem(NEWTON, HALO, 1, ROWS, 128), vmem(NEWTON, HALO, 1, ROWS, 128),
        vmem(NEWTON, 2 * depth, *TILE), vmem(NEWTON, 2 * depth, *TILE), vmem(NEWTON, 2 * depth, *TILE),
        vmem(NEWTON, 2, pz, *TILE), vmem(NEWTON, pz, ROWS, 128), vmem(NEWTON, pz, ROWS, 128),
        vmem(NEWTON, 8, *TILE), vmem(NEWTON, 3, gyn, 8, *TILE), vmem(NEWTON, *TILE), vmem(NEWTON, 3, gyn, *TILE),
        vmem(8, ROWS, 128 * gyn), vmem(ROWS, 128), vmem(gyn, ROWS, 128),
        vmem(NEWTON, *TILE), vmem(NEWTON, gyn, *TILE), vmem(NEWTON, gxn, *TILE), vmem(NEWTON, *TILE),
        dma(8), dma(8), dma(NEWTON, HALO, 8), dma(NEWTON, HALO, 8), dma(NEWTON, 8), dma(NEWTON, 8),
        dma(NEWTON, 3, gyn), dma(NEWTON, 3, gyn), dma(NEWTON, 3, gyn), dma(NEWTON, 3, gyn),
        dma(NEWTON, gyn), dma(NEWTON, gyn), dma(NEWTON, gxn), dma(NEWTON, gxn),
    ]
    return pl.pallas_call(
        functools.partial(kernel, gxn, gyn, depth),
        out_shape=jax.ShapeDtypeStruct(args[0].shape, jnp.float32),
        in_specs=[pl.BlockSpec(memory_space=pltpu.VMEM)] * 4 + [pl.BlockSpec(memory_space=pltpu.SMEM)] * 4,
        out_specs=pl.BlockSpec(memory_space=pltpu.VMEM),
        scratch_shapes=scratch,
        compiler_params=pltpu.CompilerParams(
            collective_id=0, has_side_effects=True, vmem_limit_bytes=40 * 1024 * 1024),
    )(*args)


def solution(mesh):
    cells = P(None, "gx", "gy")
    placed = (cells, cells, cells, P("gx", "gy"), P(), P(), P(), P())
    return jax.shard_map(
        functools.partial(on_device, mesh.shape["gx"], mesh.shape["gy"]),
        mesh=mesh, in_specs=placed, out_specs=cells, check_vma=False,
    )
```

time: 1310 us -> 138 us (0.11)
  blocking collectives: 601 us -> 0 us
  starting transfers between devices: 350 us -> 0 us
  waiting for transfers between devices: 238 us -> 0 us
  Pallas kernels: 0 us -> 131 us
  local copies, waits for them, and re-layouts: 50.8 us -> 6.26 us
  other arithmetic: 34.8 us -> 0 us
  between operations: 22.8 us -> 0.02 us
    psum x12 -> x0, blocking collectives: 493 us -> none  [the longest x6 244 us: on_device(): product = lax.psum(jnp.sum(basis[index] * image), ('gx', 'gy'))]
    ppermute x152 -> x0, starting transfers between devices: 350 us -> none  [the longest x76 251 us: padded_2(): lax.ppermute(tail, axis, [(i, (i + 1) % count) for i in range(ends)])]
    ppermute x152 -> x0, waiting for transfers between devices: 238 us -> none  [the longest x76 234 us: padded_2(): lax.ppermute(head, axis, [((i + 1) % count, i) for i in range(ends)])]
    pallas_call x0 -> x1, Pallas kernels: none -> 131 us  [on_device(): pl.pallas_call(functools.partial(kernel, gxn, gyn, depth), out_shape=jax....]
    all_gather x18 -> x0, blocking collectives: 109 us -> none  [the longest x4 27.3 us: coarse_solve(): whole = lax.all_gather(rhs_coarse, 'gy', axis=2, tiled=True)]
    slice x148 -> x0, local copies, waits for them, and re-layouts: 18.8 us -> none  [the longest x8 8.16 us: restrict(): parts[:, :, 0, :, 1]]
    reduce_sum x18 -> x0, other arithmetic: 14.6 us -> none  [the longest x4 6.4 us: on_device(): jnp.sum(image * image)]
  transfers between devices with their start and end apart: 152 -> 0, of which waited for: 83 -> 0; matrix products, arithmetic and copies ran while one was open for 1% -> 0% of each run, Pallas kernels for 0% -> 0%
where the time goes in v1:
time: 138 us; the launch traced here: 137 us
  Pallas kernels  131 us (95%)
  local copies, waits for them, and re-layouts  6.26 us (5%)
    pallas_call x1, Pallas kernels, on_device(): pl.pallas_call(functools.partial(kernel, gxn, gyn, depth), out_shape=jax....  131 us
    unnamed x17, local copies, waits for them, and re-layouts  6.26 us

profile of v1, /device:TPU:0, one launch (start us, length us, event | category | flops | bytes accessed | tf_op | source)
XLA Modules:
  0.0 137.1 jit_solution(3198985058626741150)
XLA Ops:
  0.0 0.0 copy-start
  0.0 0.8 copy-done
  0.8 0.0 copy-start.1
  0.8 0.8 copy-done.1
  1.6 0.0 copy-start.2
  1.6 0.8 copy-done.2
  2.3 0.0 copy-start.3
  2.3 0.7 copy-done.3
  3.0 0.0 copy-start.4
  3.0 0.7 copy-done.4
  3.7 0.0 copy-start.5
  3.7 0.7 copy-done.5
  4.3 0.0 copy-start.6
  4.3 0.7 copy-done.6
  5.0 0.0 copy-start.7
  5.0 0.7 copy-done.7
  5.6 130.9 %shard_map.82 = f32[10,8,128]{2,1,0:T(8,128)S(1)} custom-call(f32[10,8,128]{2,1,0:T(8,128)S(1)} %copy-done, f32[10,8,128]{2,1,0:T(8,128)S(1)} %copy-done.1, s32[10,8,128]{2,1,0:T(8,128)S(1)} %copy-done.2, f32[8,128]{1,0:T(8,128)S(1)} %copy-done.3, f32[24]{0:T(128)S(1)} %copy-done.4, f32[24]{0:T(128)S(1)} %copy-done.5, f32[24]{0:T(128)S(1)} %copy-done.6, ...), custom_call_target="tpu_custom_call" | custom-call | tf_op jit(solution)/shard_map/pallas_call | solution.py:560
  136.5 0.6 copy.10
Async XLA Ops:
  0.0 0.8 copy-start
  0.8 0.8 copy-start.1
  1.6 0.8 copy-start.2
  2.3 0.7 copy-start.3
  3.0 0.7 copy-start.4
  3.7 0.7 copy-start.5
  4.3 0.7 copy-start.6
  5.0 0.7 copy-start.7

commit v2 on v1

--- a/solution.py
+++ b/solution.py
@@ -192,7 +192,7 @@
         def step(k, carry):
             body(k)
             return carry
-        lax.fori_loop(0, count, step, 0)
+        lax.fori_loop(0, count, step, 0, unroll=True)
 
     def stage(k):
         msg0[k] = pressure[k]
@@ -266,7 +266,7 @@
             msg[nt, turn, k] = mix
             put_edges(pack.at[nt, turn], k, mix)
             return jnp.where(slot8 == k, total, packed)
-        packed = lax.fori_loop(0, depth, deep, jnp.zeros(TILE, jnp.float32))
+        packed = lax.fori_loop(0, depth, deep, jnp.zeros(TILE, jnp.float32), unroll=True)
         if first_of_step:
             coarse_out[nt, 7] = packed
             coarse_in[nt, 1, gy] = coarse_out[nt]
@@ -325,7 +325,7 @@
             total = total + strip[4] * roll(e, 4, 1) + strip[5] * roll(e, -4, 1)
             total = total + strip[6] * below + strip[7] * above
             return e + strip[1] * total
-        e2 = lax.fori_loop(0, COARSE_SWEEPS, coarse_sweep, jnp.concatenate([mean] * gyn, axis=1))
+        e2 = lax.fori_loop(0, COARSE_SWEEPS, coarse_sweep, jnp.concatenate([mean] * gyn, axis=1), unroll=True)
         for y in range(gyn):
             solved[y] = e2[:, 128 * y:128 * (y + 1)]
         right = jnp.where(lane24 < 64, solved[jnp.minimum(gy + 1, gyn - 1)], solved[jnp.maximum(gy - 1, 0)])
@@ -428,7 +428,7 @@
             msg[nt, 1, k] = diff
             put_edges(pack.at[nt, 1], k, diff)
             return gg + mine * mine, gp + mine * diff, pp + diff * diff
-        gg, gp, pp = lax.fori_loop(0, depth, image, (zeros, zeros, zeros))
+        gg, gp, pp = lax.fori_loop(0, depth, image, (zeros, zeros, zeros), unroll=True)
         halo = halo_copies(msg.at[nt, 1], pack.at[nt, 1], recv_w.at[nt, 1], recv_e.at[nt, 1],
                            recv_n.at[nt, 1], recv_s.at[nt, 1], sh.at[nt, 1], rh.at[nt, 1])
         start(halo)
@@ -450,7 +450,7 @@
             msgz[nt, depth + k] = u
             put_edges(packz.at[nt], depth + k, u)
             return gs + mine * im, ps + own[k] * im, ss + im * im
-        gs, ps, ss = lax.fori_loop(0, depth, second, (zeros, zeros, zeros))
+        gs, ps, ss = lax.fori_loop(0, depth, second, (zeros, zeros, zeros), unroll=True)
 
         rows = [jnp.sum(item, axis=0, keepdims=True) for item in (gg, gp, pp, gs, ps, ss)]
         tile = zeros

time: 138 us -> 91.9 us (0.67)
  Pallas kernels: 131 us -> 85.2 us
    pallas_call x1, Pallas kernels: 131 us -> 85.2 us  [on_device(): pl.pallas_call(functools.partial(kernel, gxn, gyn, depth), out_shape=jax....]
where the time goes in v2:
time: 91.9 us; the launch traced here: 91.5 us
  Pallas kernels  85.2 us (93%)
  local copies, waits for them, and re-layouts  6.26 us (7%)
    pallas_call x1, Pallas kernels, on_device(): pl.pallas_call(functools.partial(kernel, gxn, gyn, depth), out_shape=jax....  85.2 us
    unnamed x17, local copies, waits for them, and re-layouts  6.26 us

profile of v2, /device:TPU:0, one launch (start us, length us, event | category | flops | bytes accessed | tf_op | source)
XLA Modules:
  0.0 91.5 jit_solution(12293388417369470051)
XLA Ops:
  0.0 0.0 copy-start
  0.0 0.8 copy-done
  0.8 0.0 copy-start.1
  0.8 0.8 copy-done.1
  1.6 0.0 copy-start.2
  1.6 0.8 copy-done.2
  2.3 0.0 copy-start.3
  2.3 0.7 copy-done.3
  3.0 0.0 copy-start.4
  3.0 0.7 copy-done.4
  3.7 0.0 copy-start.5
  3.7 0.7 copy-done.5
  4.3 0.0 copy-start.6
  4.3 0.7 copy-done.6
  5.0 0.0 copy-start.7
  5.0 0.7 copy-done.7
  5.6 85.2 %shard_map.82 = f32[10,8,128]{2,1,0:T(8,128)S(1)} custom-call(f32[10,8,128]{2,1,0:T(8,128)S(1)} %copy-done, f32[10,8,128]{2,1,0:T(8,128)S(1)} %copy-done.1, s32[10,8,128]{2,1,0:T(8,128)S(1)} %copy-done.2, f32[8,128]{1,0:T(8,128)S(1)} %copy-done.3, f32[24]{0:T(128)S(1)} %copy-done.4, f32[24]{0:T(128)S(1)} %copy-done.5, f32[24]{0:T(128)S(1)} %copy-done.6, ...), custom_call_target="tpu_custom_call" | custom-call | tf_op jit(solution)/shard_map/pallas_call | solution.py:560
  90.9 0.6 copy.10
Async XLA Ops:
  0.0 0.8 copy-start
  0.8 0.8 copy-start.1
  1.6 0.8 copy-start.2
  2.3 0.7 copy-start.3
  3.0 0.7 copy-start.4
  3.7 0.7 copy-start.5
  4.3 0.7 copy-start.6
  5.0 0.7 copy-start.7

commit v3 on v2

--- a/solution.py
+++ b/solution.py
@@ -18,7 +18,7 @@
 TILE = (8, 128)
 MESH = pl.DeviceIdType.MESH
 DIRECTIONS = tuple((dx, dy) for dx in (-1, 0, 1) for dy in (-1, 0, 1) if (dx, dy) != (0, 0))
-HALO = 3
+HALO = 5
 
 
 def roll(field, shift, axis):
@@ -68,16 +68,16 @@
 
 def kernel(
     gxn, gyn, depth,
-    pressure, saturation_old, soil_type, recharge, ksat, alpha_t, porosity_t, residual_t,
+    pressure, saturation_old, soil_type, recharge, ksat_in, alpha_in, porosity_in, residual_in,
     out,
     old, state, sat, con, alp, por, res, rch, rel,
     lev0, lev1, g, b0, xa, xb, b1, ya, yb, z0,
+    soil, ksat, alpha_t, porosity_t, residual_t,
     own, msg0, recv0_w, recv0_e, pack0, recv0_n, recv0_s,
     msg, recv_w, recv_e, pack, recv_n, recv_s,
-    msgz, recvz_w, recvz_e, packz, recvz_n, recvz_s,
     coarse_out, coarse_in, rhs_out, rhs_in, strip, strip_sum, solved,
     part_out, part_y, part_x, whole_x,
-    s0, r0, sh, rh, sz, rz, sc, rc, sb, rb, sy, ry, sx, rx,
+    local, s0, r0, sh, rh, sc, rc, sb, rb, sy, ry, sx, rx,
 ):
     gx, gy = lax.axis_index("gx"), lax.axis_index("gy")
     has_w, has_e = gx > 0, gx < gxn - 1
@@ -91,8 +91,20 @@
     def place(dx, dy):
         return (jnp.clip(gx + dx, 0, gxn - 1), jnp.clip(gy + dy, 0, gyn - 1))
 
+    assert depth % 2 == 0
+    half = depth // 2
+    fetches = [
+        pltpu.make_async_copy(src, dst, local.at[i])
+        for i, (src, dst) in enumerate((
+            (soil_type, soil), (pressure, msg0.at[1, pl.ds(0, depth)]),
+            (saturation_old, msg0.at[2, pl.ds(0, depth)]), (recharge, msg0.at[2, depth]),
+            (ksat_in, ksat), (alpha_in, alpha_t), (porosity_in, porosity_t), (residual_in, residual_t)))
+    ]
+    for fetch in fetches:
+        fetch.start()
+
     for ref in (recv0_w, recv0_e, recv0_n, recv0_s, recv_w, recv_e, recv_n, recv_s,
-                recvz_w, recvz_e, recvz_n, recvz_s, coarse_in, rhs_in, pack0, pack, packz):
+                coarse_in, rhs_in, pack0, pack):
         ref[...] = jnp.zeros(ref.shape, ref.dtype)
 
     barrier = pltpu.get_barrier_semaphore()
@@ -108,7 +120,6 @@
         def _():
             pl.semaphore_signal(barrier, inc=1, device_id=(x, gy), device_id_type=MESH)
     strips = 1 + has_w.astype(jnp.int32) + has_e.astype(jnp.int32)
-    pl.semaphore_wait(barrier, gyn * strips - 1 + gxn - strips)
 
     lane8, row8 = iota(TILE, 1), iota(TILE, 0)
     slot8 = (row8 & 3) * 4 + (lane8 & 3)
@@ -194,39 +205,58 @@
             return carry
         lax.fori_loop(0, count, step, 0, unroll=True)
 
+    def first_copies(group, count):
+        rows = pl.ds(0, count)
+        return halo_copies(msg0.at[group, rows], pack0.at[group], recv0_w.at[group, rows], recv0_e.at[group, rows],
+                           recv0_n.at[group], recv0_s.at[group], s0.at[group], r0.at[group])
+
+    def first_ext(group, k):
+        return extended(k, msg0[group, k], recv0_w.at[group], recv0_e.at[group], recv0_n.at[group], recv0_s.at[group])
+
+    fetches[0].wait()
+
     def stage(k):
-        msg0[k] = pressure[k]
-        msg0[depth + k] = saturation_old[k]
-        msg0[2 * depth + k] = soil_type[k].astype(jnp.float32)
+        msg0[0, k] = soil[k].astype(jnp.float32)
+        put_edges(pack0.at[0], k, msg0[0, k])
     layers(stage)
-    msg0[3 * depth] = recharge[...]
-    layers(lambda k: put_edges(pack0, k, msg0[k]), 3 * depth + 1)
-    first = halo_copies(msg0, pack0, recv0_w, recv0_e, recv0_n, recv0_s, s0, r0)
-    start(first)
-    arrive(first)
+    for fetch in fetches[1:]:
+        fetch.wait()
+    layers(lambda k: put_edges(pack0.at[1], k, msg0[1, k]))
+    layers(lambda k: put_edges(pack0.at[2], k, msg0[2, k]), depth + 1)
+    pl.semaphore_wait(barrier, gyn * strips - 1 + gxn - strips)
+    groups = [first_copies(0, depth), first_copies(1, depth), first_copies(2, depth + 1)]
+    for group in groups:
+        start(group)
 
     valid = (
         ((row_e >= 8) | has_w) & ((row_e < 16) | has_e)
         & ((lane_e < 128) | ((lane_e < 136) & has_n) | ((lane_e >= 248) & has_s))
     )
-
-    def first_ext(k):
-        return extended(k, msg0[k], recv0_w, recv0_e, recv0_n, recv0_s)
-
-    def unpack_inputs(k):
-        old[k] = first_ext(k)
-        state[k] = old[k]
-        sat[k] = first_ext(depth + k)
-        soil = first_ext(2 * depth + k)
+    arrive(groups[0])
+
+    def look_up(k):
+        kinds = first_ext(0, k)
         values = [jnp.zeros((ROWS, LANES), jnp.float32) for _ in range(4)]
         for kind in range(ksat.shape[0]):
-            here = soil == float(kind)
+            here = kinds == float(kind)
             values = [jnp.where(here, table[kind], value) for table, value in zip((ksat, alpha_t, porosity_t, residual_t), values)]
         con[k] = jnp.where(valid, values[0], 0.0)
         alp[k], por[k], res[k] = values[1], values[2], values[3]
-    layers(unpack_inputs)
-    rch[...] = first_ext(3 * depth)
-    sent(first)
+    layers(look_up)
+    arrive(groups[1])
+
+    def unpack_pressure(k):
+        old[k] = first_ext(1, k)
+        state[k] = old[k]
+    layers(unpack_pressure)
+    arrive(groups[2])
+
+    def unpack_saturation(k):
+        sat[k] = first_ext(2, k)
+    layers(unpack_saturation)
+    rch[...] = first_ext(2, depth)
+    for group in groups:
+        sent(group)
 
     def pulled(level, ref, k, field, step):
         total = level[2, k] * roll(field, step, 0) + level[3, k] * roll(field, -step, 0)
@@ -244,7 +274,16 @@
             dst[k] = field + level[1, k] * left
         layers(body)
 
-    def precondition(nt, j, rhs, gathers, received, first_of_step):
+    def round_copies(nt, turn, count):
+        rows = pl.ds(0, count)
+        return halo_copies(msg.at[nt, turn, rows], pack.at[nt, turn], recv_w.at[nt, turn, rows], recv_e.at[nt, turn, rows],
+                           recv_n.at[nt, turn], recv_s.at[nt, turn], sh.at[nt, turn], rh.at[nt, turn])
+
+    def round_ext(nt, turn, k):
+        return extended(k, msg[nt, turn, k], recv_w.at[nt, turn], recv_e.at[nt, turn],
+                        recv_n.at[nt, turn], recv_s.at[nt, turn])
+
+    def precondition(nt, j, rhs, operator):
         def begin(k):
             xa[k] = lev0[1, k] * rhs[k]
         layers(begin)
@@ -259,25 +298,25 @@
         sweep(lev1, ya, b1, yb, 2)
         turn = 2 * j
 
+        def stage_middle(i):
+            pair_of = []
+            for k in (i, i + half):
+                pair_of.append(jnp.where((row8 & 1) == 0, yb[k][8:16, :128], b1[k][8:16, :128]))
+            mix = jnp.where((lane8 & 1) == 0, pair_of[0], pair_of[1])
+            msg[nt, turn, i] = mix
+            put_edges(pack.at[nt, turn], i, mix)
+        layers(stage_middle, half)
+        halo = round_copies(nt, turn, half)
+        start(halo)
+
         def deep(k, packed):
-            field, left = residual(lev1, yb, b1, k, 2)
-            total = sum_four(left[8:16, :128], 2)
-            mix = jnp.where((row8 & 1) == 0, field[8:16, :128], b1[k][8:16, :128])
-            msg[nt, turn, k] = mix
-            put_edges(pack.at[nt, turn], k, mix)
-            return jnp.where(slot8 == k, total, packed)
+            _, left = residual(lev1, yb, b1, k, 2)
+            return jnp.where(slot8 == k, sum_four(left[8:16, :128], 2), packed)
         packed = lax.fori_loop(0, depth, deep, jnp.zeros(TILE, jnp.float32), unroll=True)
-        if first_of_step:
-            coarse_out[nt, 7] = packed
-            coarse_in[nt, 1, gy] = coarse_out[nt]
-        else:
-            rhs_out[nt] = packed
-            rhs_in[nt, 1, gy] = packed
-        halo = halo_copies(msg.at[nt, turn], pack.at[nt, turn], recv_w.at[nt, turn], recv_e.at[nt, turn],
-                           recv_n.at[nt, turn], recv_s.at[nt, turn], sh.at[nt, turn], rh.at[nt, turn])
+        rhs_out[nt, j] = packed
+        rhs_in[nt, j, 1, gy] = packed
+        gathers = gather_copies(rhs_out.at[nt, j], rhs_in.at[nt, j], sb.at[nt, j], rb.at[nt, j])
         start(gathers)
-        start(halo)
-        arrive(gathers)
 
         def strips_of(pick):
             return jnp.concatenate(
@@ -294,36 +333,35 @@
                 total = total + roll(total, step, 1)
             return sum_pair(total, 4, 0)
 
-        if first_of_step:
-            parts = [strips_of(lambda s, y: coarse_in[nt, s, y, f]) for f in range(7)]
-            diag = parts[0]
-            for part in parts[1:]:
-                diag = diag + part
+        def beneath(e):
+            return jnp.where((wide_lane & 3) == 0, roll(roll(e, 1, 0), -3, 1), roll(e, 1, 1))
+
+        def over(e):
+            return jnp.where((wide_lane & 3) == 3, roll(roll(e, -1, 0), 3, 1), roll(e, -1, 1))
+
+        if operator is not None:
+            arrive(operator)
+            diag, south, lower, mixed = (strips_of(lambda s, y: coarse_in[nt, s, y, f]) for f in range(4))
             live = diag > 0.0
+            first_row = (wide_row & 4) == 0
             strip[0] = diag
             strip[1] = jnp.where(live, OMEGA / jnp.where(live, diag, 1.0), 0.0)
-            half = (wide_row & 4) == 0
-            strip[2] = jnp.where(half, 0.0, parts[1])
-            strip[3] = jnp.where(half, parts[2], 0.0)
-            for f in range(3, 7):
-                strip[f + 1] = parts[f]
-            strip_sum[...] = strip_totals(parts[0])
-            b2 = strips_of(lambda s, y: coarse_in[nt, s, y, 7])
-        else:
-            b2 = strips_of(lambda s, y: rhs_in[nt, s, y])
+            strip[2] = jnp.where(first_row, 0.0, roll(mixed, 4, 0))
+            strip[3] = jnp.where(first_row, mixed, 0.0)
+            strip[4], strip[5] = south, roll(south, -4, 1)
+            strip[6], strip[7] = lower, over(lower)
+            strip_sum[...] = strip_totals(jnp.where(first_row, 0.0, mixed))
+        arrive(gathers)
+        b2 = strips_of(lambda s, y: rhs_in[nt, j, s, y])
         below_sum = strip_sum[...]
         some = below_sum > 0.0
         mean = jnp.where(some, strip_totals(b2) / jnp.where(some, below_sum, 1.0), 0.0)
 
         def coarse_sweep(_, e):
-            up1, up2 = roll(e, 1, 1), roll(roll(e, 1, 0), -3, 1)
-            below = jnp.where((wide_lane & 3) == 0, up2, up1)
-            dn1, dn2 = roll(e, -1, 1), roll(roll(e, -1, 0), 3, 1)
-            above = jnp.where((wide_lane & 3) == 3, dn2, dn1)
             total = b2 - strip[0] * e
             total = total + strip[2] * roll(e, 4, 0) + strip[3] * roll(e, -4, 0)
             total = total + strip[4] * roll(e, 4, 1) + strip[5] * roll(e, -4, 1)
-            total = total + strip[6] * below + strip[7] * above
+            total = total + strip[6] * beneath(e) + strip[7] * over(e)
             return e + strip[1] * total
         e2 = lax.fori_loop(0, COARSE_SWEEPS, coarse_sweep, jnp.concatenate([mean] * gyn, axis=1), unroll=True)
         for y in range(gyn):
@@ -333,19 +371,22 @@
         slot_e = (row_e & 3) * 4 + (lane_e & 3)
         arrive(halo)
 
-        def up(k):
-            m = jnp.where(slot_e == k, around, 0.0)
-            m = roll(m, lax.rem(LANES - (k & 3), LANES), 1)
-            m = m + roll(m, 1, 1)
-            m = m + roll(m, 2, 1)
-            m = roll(m, lax.rem(ROWS - (k >> 2), ROWS), 0)
-            m = m + roll(m, 1, 0)
-            m = m + roll(m, 2, 0)
-            mix = extended(k, msg[nt, turn, k], recv_w.at[nt, turn], recv_e.at[nt, turn],
-                           recv_n.at[nt, turn], recv_s.at[nt, turn])
-            ya[k] = m + jnp.where(even_row, mix, roll(mix, 1, 0))
-            b1[k] = jnp.where(even_row, roll(mix, -1, 0), mix)
-        layers(up)
+        def up(i):
+            mix = round_ext(nt, turn, i)
+            for k, low in ((i, True), (i + half, False)):
+                def put():
+                    m = jnp.where(slot_e == k, around, 0.0)
+                    m = roll(m, lax.rem(LANES - (k & 3), LANES), 1)
+                    m = m + roll(m, 1, 1)
+                    m = m + roll(m, 2, 1)
+                    m = roll(m, lax.rem(ROWS - (k >> 2), ROWS), 0)
+                    m = m + roll(m, 1, 0)
+                    m = m + roll(m, 2, 0)
+                    both = spread_low(mix, 1, 1) if low else spread_high(mix, 1, 1)
+                    ya[k] = m + jnp.where(even_row, both, roll(both, 1, 0))
+                    b1[k] = jnp.where(even_row, roll(both, -1, 0), both)
+                put()
+        layers(up, half)
         sweep(lev1, ya, b1, yb, 2)
 
         def join(k):
@@ -384,7 +425,7 @@
             lev0[6, k] = jnp.where(k > 0, lower, 0.0)
         layers(faces)
 
-        def operators(k):
+        def operators(k, packed):
             west, east, south, north, lower = (lev0[f, k] for f in range(2, 7))
             upper = jnp.where(k < last, lev0[6, jnp.minimum(k + 1, last)], 0.0)
             lev0[7, k] = upper
@@ -406,14 +447,19 @@
                 diag = diag + middle[f]
             lev1[0, k], lev1[1, k] = diag, OMEGA / diag
             coarse = coarsen([field[8:16, :128] for field in middle], 2)
-            for f in range(7):
-                coarse_out[nt, f] = jnp.where(slot8 == k, coarse[f], coarse_out[nt, f])
-        for f in range(7):
-            coarse_out[nt, f] = jnp.zeros(TILE, jnp.float32)
-        layers(operators)
-
-        coarse = gather_copies(coarse_out.at[nt], coarse_in.at[nt], sc.at[nt], rc.at[nt])
-        precondition(nt, 0, g, coarse, coarse_in, True)
+            diag = coarse[0]
+            for f in range(1, 7):
+                diag = diag + coarse[f]
+            mixed = jnp.where((row8 & 4) == 0, coarse[2], sum_pair(coarse[0], 4, 0))
+            return tuple(jnp.where(slot8 == k, field, so_far)
+                         for field, so_far in zip((diag, coarse[3], coarse[5], mixed), packed))
+        packed = lax.fori_loop(0, depth, operators, (jnp.zeros(TILE, jnp.float32),) * 4, unroll=True)
+        for f in range(4):
+            coarse_out[nt, f] = packed[f]
+            coarse_in[nt, 1, gy, f] = packed[f]
+        operator = gather_copies(coarse_out.at[nt], coarse_in.at[nt], sc.at[nt], rc.at[nt])
+        start(operator)
+        precondition(nt, 0, g, operator)
 
         zeros = jnp.zeros(TILE, jnp.float32)
 
@@ -422,33 +468,36 @@
             mine = g[k][8:16, :128]
             diff = applied(k) - mine
             z0[k] = xb[k][8:16, :128]
-            msgz[nt, k] = z0[k]
-            put_edges(packz.at[nt], k, z0[k])
+            msg[nt, 3, k] = z0[k]
+            put_edges(pack.at[nt, 3], k, z0[k])
             own[k] = diff
             msg[nt, 1, k] = diff
             put_edges(pack.at[nt, 1], k, diff)
             return gg + mine * mine, gp + mine * diff, pp + diff * diff
         gg, gp, pp = lax.fori_loop(0, depth, image, (zeros, zeros, zeros), unroll=True)
-        halo = halo_copies(msg.at[nt, 1], pack.at[nt, 1], recv_w.at[nt, 1], recv_e.at[nt, 1],
-                           recv_n.at[nt, 1], recv_s.at[nt, 1], sh.at[nt, 1], rh.at[nt, 1])
+        halo = round_copies(nt, 1, depth)
+        halo_z = round_copies(nt, 3, depth)
+        halo_u = round_copies(nt, 4, depth)
         start(halo)
         arrive(halo)
 
+        @pl.when(nt < NEWTON - 1)
+        def _():
+            start(halo_z)
+
         def spread(k):
-            b0[k] = extended(k, own[k], recv_w.at[nt, 1], recv_e.at[nt, 1], recv_n.at[nt, 1], recv_s.at[nt, 1])
+            b0[k] = round_ext(nt, 1, k)
         layers(spread)
         sent(halo)
-
-        right_sides = gather_copies(rhs_out.at[nt], rhs_in.at[nt], sb.at[nt], rb.at[nt])
-        precondition(nt, 1, b0, right_sides, rhs_in, False)
+        precondition(nt, 1, b0, None)
 
         def second(k, sums):
             gs, ps, ss = sums
             mine = g[k][8:16, :128]
             im = applied(k)
             u = xb[k][8:16, :128]
-            msgz[nt, depth + k] = u
-            put_edges(packz.at[nt], depth + k, u)
+            msg[nt, 4, k] = u
+            put_edges(pack.at[nt, 4], k, u)
             return gs + mine * im, ps + own[k] * im, ss + im * im
         gs, ps, ss = lax.fori_loop(0, depth, second, (zeros, zeros, zeros), unroll=True)
 
@@ -459,12 +508,10 @@
         part_out[nt] = tile
         along_y = sum_copies(part_out.at[nt], part_y.at[nt], sy.at[nt], ry.at[nt], gyn, False)
         start(along_y)
-        basis = halo_copies(msgz.at[nt], packz.at[nt], recvz_w.at[nt], recvz_e.at[nt],
-                            recvz_n.at[nt], recvz_s.at[nt], sz.at[nt], rz.at[nt])
 
         @pl.when(nt < NEWTON - 1)
         def _():
-            start(basis)
+            start(halo_u)
         arrive(along_y)
         for j in range(1, gyn):
             tile = tile + part_y[nt, j]
@@ -505,21 +552,22 @@
 
         @pl.when(nt < NEWTON - 1)
         def _():
-            arrive(basis)
+            arrive(halo_z)
+            arrive(halo_u)
 
             def advance(k):
-                z = extended(k, z0[k], recvz_w.at[nt], recvz_e.at[nt], recvz_n.at[nt], recvz_s.at[nt])
-                u = extended(depth + k, msgz[nt, depth + k], recvz_w.at[nt], recvz_e.at[nt], recvz_n.at[nt], recvz_s.at[nt])
-                state[k] = state[k] + first_weight * z + second_weight * u
+                state[k] = state[k] + first_weight * round_ext(nt, 3, k) + second_weight * round_ext(nt, 4, k)
             layers(advance)
-            sent(basis)
+            sent(halo_z)
+            sent(halo_u)
 
         @pl.when(nt == NEWTON - 1)
         def _():
             def finish(k):
                 out[k] = (state[k][8:16, :128] + first_weight[:, :128] * z0[k]
-                          + second_weight[:, :128] * msgz[nt, depth + k])
+                          + second_weight[:, :128] * msg[nt, 4, k])
             layers(finish)
+        sent(operator)
         sent(along_y)
         sent(along_x)
         return carry
@@ -538,29 +586,27 @@
 
     ext = vmem(depth, ROWS, LANES)
     level = vmem(8, depth, ROWS, LANES)
-    n0 = 3 * depth + 1
-    p0 = (n0 + 15) // 16
-    pz = (2 * depth + 15) // 16
+    n0 = depth + 1
+    assert n0 <= 16
     scratch = [ext] * 7 + [vmem(ROWS, LANES), ext]
     scratch += [level, level] + [ext] * 7 + [vmem(depth, *TILE)]
+    scratch += [pltpu.VMEM((depth,) + TILE, jnp.int32)] + [pltpu.SMEM(item.shape, jnp.float32) for item in args[4:]]
     scratch += [
-        vmem(depth, *TILE), vmem(n0, *TILE), vmem(n0, *TILE), vmem(n0, *TILE),
-        vmem(2, p0, *TILE), vmem(p0, ROWS, 128), vmem(p0, ROWS, 128),
+        vmem(depth, *TILE), vmem(3, n0, *TILE), vmem(3, n0, *TILE), vmem(3, n0, *TILE),
+        vmem(3, 2, 1, *TILE), vmem(3, 1, ROWS, 128), vmem(3, 1, ROWS, 128),
         vmem(NEWTON, HALO, depth, *TILE), vmem(NEWTON, HALO, depth, *TILE), vmem(NEWTON, HALO, depth, *TILE),
         vmem(NEWTON, HALO, 2, 1, *TILE), vmem(NEWTON, HALO, 1, ROWS, 128), vmem(NEWTON, HALO, 1, ROWS, 128),
-        vmem(NEWTON, 2 * depth, *TILE), vmem(NEWTON, 2 * depth, *TILE), vmem(NEWTON, 2 * depth, *TILE),
-        vmem(NEWTON, 2, pz, *TILE), vmem(NEWTON, pz, ROWS, 128), vmem(NEWTON, pz, ROWS, 128),
-        vmem(NEWTON, 8, *TILE), vmem(NEWTON, 3, gyn, 8, *TILE), vmem(NEWTON, *TILE), vmem(NEWTON, 3, gyn, *TILE),
+        vmem(NEWTON, 4, *TILE), vmem(NEWTON, 3, gyn, 4, *TILE), vmem(NEWTON, 2, *TILE), vmem(NEWTON, 2, 3, gyn, *TILE),
         vmem(8, ROWS, 128 * gyn), vmem(ROWS, 128), vmem(gyn, ROWS, 128),
         vmem(NEWTON, *TILE), vmem(NEWTON, gyn, *TILE), vmem(NEWTON, gxn, *TILE), vmem(NEWTON, *TILE),
-        dma(8), dma(8), dma(NEWTON, HALO, 8), dma(NEWTON, HALO, 8), dma(NEWTON, 8), dma(NEWTON, 8),
-        dma(NEWTON, 3, gyn), dma(NEWTON, 3, gyn), dma(NEWTON, 3, gyn), dma(NEWTON, 3, gyn),
+        dma(8), dma(3, 8), dma(3, 8), dma(NEWTON, HALO, 8), dma(NEWTON, HALO, 8),
+        dma(NEWTON, 3, gyn), dma(NEWTON, 3, gyn), dma(NEWTON, 2, 3, gyn), dma(NEWTON, 2, 3, gyn),
         dma(NEWTON, gyn), dma(NEWTON, gyn), dma(NEWTON, gxn), dma(NEWTON, gxn),
     ]
     return pl.pallas_call(
         functools.partial(kernel, gxn, gyn, depth),
         out_shape=jax.ShapeDtypeStruct(args[0].shape, jnp.float32),
-        in_specs=[pl.BlockSpec(memory_space=pltpu.VMEM)] * 4 + [pl.BlockSpec(memory_space=pltpu.SMEM)] * 4,
+        in_specs=[pl.BlockSpec(memory_space=pl.ANY)] * 8,
         out_specs=pl.BlockSpec(memory_space=pltpu.VMEM),
         scratch_shapes=scratch,
         compiler_params=pltpu.CompilerParams(

time: 91.9 us -> 85.6 us (0.931)
  Pallas kernels: 85.2 us -> 78.9 us
    pallas_call x1, Pallas kernels: 85.2 us -> 78.9 us  [on_device(): pl.pallas_call(functools.partial(kernel, gxn, gyn, depth), out_shape=jax....]
where the time goes in v3:
time: 85.6 us; the launch traced here: 85.2 us
  Pallas kernels  78.9 us (92%)
  local copies, waits for them, and re-layouts  6.26 us (7%)
    pallas_call x1, Pallas kernels, on_device(): pl.pallas_call(functools.partial(kernel, gxn, gyn, depth), out_shape=jax....  78.9 us
    unnamed x17, local copies, waits for them, and re-layouts  6.26 us

profile of v3, /device:TPU:0, one launch (start us, length us, event | category | flops | bytes accessed | tf_op | source)
XLA Modules:
  0.0 85.2 jit_solution(340382657665261619)
XLA Ops:
  0.0 0.0 copy-start
  0.0 0.8 copy-done
  0.8 0.0 copy-start.1
  0.8 0.8 copy-done.1
  1.6 0.0 copy-start.2
  1.6 0.8 copy-done.2
  2.3 0.0 copy-start.3
  2.3 0.7 copy-done.3
  3.0 0.0 copy-start.4
  3.0 0.7 copy-done.4
  3.7 0.0 copy-start.5
  3.7 0.7 copy-done.5
  4.3 0.0 copy-start.6
  4.3 0.7 copy-done.6
  5.0 0.0 copy-start.7
  5.0 0.7 copy-done.7
  5.6 78.9 %shard_map.82 = f32[10,8,128]{2,1,0:T(8,128)S(1)} custom-call(f32[10,8,128]{2,1,0:T(8,128)S(1)} %copy-done, f32[10,8,128]{2,1,0:T(8,128)S(1)} %copy-done.1, s32[10,8,128]{2,1,0:T(8,128)S(1)} %copy-done.2, f32[8,128]{1,0:T(8,128)S(1)} %copy-done.3, f32[24]{0:T(128)S(1)} %copy-done.4, f32[24]{0:T(128)S(1)} %copy-done.5, f32[24]{0:T(128)S(1)} %copy-done.6, ...), custom_call_target="tpu_custom_call" | custom-call | tf_op jit(solution)/shard_map/pallas_call | solution.py:606
  84.6 0.6 copy.10
Async XLA Ops:
  0.0 0.8 copy-start
  0.8 0.8 copy-start.1
  1.6 0.8 copy-start.2
  2.3 0.7 copy-start.3
  3.0 0.7 copy-start.4
  3.7 0.7 copy-start.5
  4.3 0.7 copy-start.6
  5.0 0.7 copy-start.7

commit v4 on v3

--- a/solution.py
+++ b/solution.py
@@ -70,7 +70,7 @@
     gxn, gyn, depth,
     pressure, saturation_old, soil_type, recharge, ksat_in, alpha_in, porosity_in, residual_in,
     out,
-    old, state, sat, con, alp, por, res, rch, rel,
+    old, state, sat, con, alp, por, res, rch, rel, stored,
     lev0, lev1, g, b0, xa, xb, b1, ya, yb, z0,
     soil, ksat, alpha_t, porosity_t, residual_t,
     own, msg0, recv0_w, recv0_e, pack0, recv0_n, recv0_s,
@@ -103,6 +103,10 @@
     for fetch in fetches:
         fetch.start()
 
+    for ref in (xa, xb, ya, yb):
+        for h in range(2):
+            ref[h, pl.ds(0, 8)] = jnp.zeros(TILE, jnp.float32)
+            ref[h, pl.ds(8 + ROWS * depth, 8)] = jnp.zeros(TILE, jnp.float32)
     for ref in (recv0_w, recv0_e, recv0_n, recv0_s, recv_w, recv_e, recv_n, recv_s,
                 coarse_in, rhs_in, pack0, pack):
         ref[...] = jnp.zeros(ref.shape, ref.dtype)
@@ -128,12 +132,12 @@
     even_row = (row_e & 1) == 0
 
     def put_edges(packs, k, block):
-        at = lax.rem(k, 16)
+        at = (k % 16)
         moved = roll(block, at * 8, 1)
         group = lane8 >> 3
         where = k // 16
         packs[0, where] = jnp.where(group == at, moved, packs[0, where])
-        packs[1, where] = jnp.where(group == lax.rem(at + 15, 16), moved, packs[1, where])
+        packs[1, where] = jnp.where(group == ((at + 15) % 16), moved, packs[1, where])
 
     def halo_copies(blocks, packs, to_w, to_e, to_n, to_s, send, recv):
         copies = []
@@ -193,17 +197,38 @@
 
     def extended(k, block, from_w, from_e, from_n, from_s):
         left = jnp.concatenate([from_w[k], block, from_e[k]], axis=0)
-        back = lax.rem(16 - lax.rem(k, 16), 16) * 8
+        back = (16 - (k % 16)) % 16 * 8
         where = k // 16
         north, south = roll(from_n[where], back, 1), roll(from_s[where], back, 1)
         right = jnp.where(lane24 < 8, north, jnp.where(lane24 >= 120, south, 0.0))
         return jnp.concatenate([left, right], axis=1)
 
     def layers(body, count=depth):
-        def step(k, carry):
+        for k in range(count):
             body(k)
-            return carry
-        lax.fori_loop(0, count, step, 0, unroll=True)
+
+    def gather_layers(body, carry):
+        for k in range(depth):
+            carry = body(k, carry)
+        return carry
+
+    def get(ref, k, low=0, count=ROWS, shift=0):
+        rows = pl.ds(8 + ROWS * k + low + shift, count)
+        return jnp.concatenate([ref[0, rows], ref[1, rows]], axis=1)
+
+    def put(ref, k, field, low=0):
+        rows = pl.ds(8 + ROWS * k + low, field.shape[0])
+        ref[0, rows] = field[:, :128]
+        ref[1, rows] = field[:, 128:]
+
+    def mine_of(ref, k):
+        return ref[0, pl.ds(8 + ROWS * k + 8, 8)]
+
+    def below_of(k):
+        return max(k - 1, 0)
+
+    def above_of(k):
+        return min(k + 1, last)
 
     def first_copies(group, count):
         rows = pl.ds(0, count)
@@ -258,20 +283,22 @@
     for group in groups:
         sent(group)
 
-    def pulled(level, ref, k, field, step):
-        total = level[2, k] * roll(field, step, 0) + level[3, k] * roll(field, -step, 0)
-        total = total + level[4, k] * roll(field, step, 1) + level[5, k] * roll(field, -step, 1)
-        below, above = ref[jnp.maximum(k - 1, 0)], ref[jnp.minimum(k + 1, last)]
-        return total + level[6, k] * below + level[7, k] * above
-
-    def residual(level, ref, rhs, k, step):
-        field = ref[k]
-        return field, rhs[k] - level[0, k] * field + pulled(level, ref, k, field, step)
-
-    def sweep(level, src, rhs, dst, step):
+    def pulled(level, ref, k, field, step, low, count):
+        faces = [get(level.at[f], k, low, count) for f in range(2, 8)]
+        total = faces[0] * get(ref, k, low, count, -step) + faces[1] * get(ref, k, low, count, step)
+        total = total + faces[2] * roll(field, step, 1) + faces[3] * roll(field, -step, 1)
+        total = total + faces[4] * get(ref, below_of(k), low, count)
+        return total + faces[5] * get(ref, above_of(k), low, count)
+
+    def residual(level, ref, rhs, k, step, low=0, count=ROWS):
+        field = get(ref, k, low, count)
+        around = pulled(level, ref, k, field, step, low, count)
+        return field, get(rhs, k, low, count) - get(level.at[0], k, low, count) * field + around
+
+    def sweep(level, src, rhs, dst, step, low=0, count=ROWS):
         def body(k):
-            field, left = residual(level, src, rhs, k, step)
-            dst[k] = field + level[1, k] * left
+            field, left = residual(level, src, rhs, k, step, low, count)
+            put(dst, k, field + get(level.at[1], k, low, count) * left, low)
         layers(body)
 
     def round_copies(nt, turn, count):
@@ -285,23 +312,23 @@
 
     def precondition(nt, j, rhs, operator):
         def begin(k):
-            xa[k] = lev0[1, k] * rhs[k]
+            put(xa, k, get(lev0.at[1], k) * get(rhs, k))
         layers(begin)
         sweep(lev0, xa, rhs, xb, 1)
 
         def down(k):
-            _, left = residual(lev0, xb, rhs, k, 1)
+            _, left = residual(lev0, xb, rhs, k, 1, 4, 16)
             total = sum_four(left, 1)
-            b1[k] = total
-            ya[k] = lev1[1, k] * total
+            put(b1, k, total, 4)
+            put(ya, k, get(lev1.at[1], k, 4, 16) * total, 4)
         layers(down)
-        sweep(lev1, ya, b1, yb, 2)
+        sweep(lev1, ya, b1, yb, 2, 4, 16)
         turn = 2 * j
 
         def stage_middle(i):
             pair_of = []
             for k in (i, i + half):
-                pair_of.append(jnp.where((row8 & 1) == 0, yb[k][8:16, :128], b1[k][8:16, :128]))
+                pair_of.append(jnp.where((row8 & 1) == 0, mine_of(yb, k), mine_of(b1, k)))
             mix = jnp.where((lane8 & 1) == 0, pair_of[0], pair_of[1])
             msg[nt, turn, i] = mix
             put_edges(pack.at[nt, turn], i, mix)
@@ -310,9 +337,9 @@
         start(halo)
 
         def deep(k, packed):
-            _, left = residual(lev1, yb, b1, k, 2)
-            return jnp.where(slot8 == k, sum_four(left[8:16, :128], 2), packed)
-        packed = lax.fori_loop(0, depth, deep, jnp.zeros(TILE, jnp.float32), unroll=True)
+            _, left = residual(lev1, yb, b1, k, 2, 8, 8)
+            return jnp.where(slot8 == k, sum_four(left[:, :128], 2), packed)
+        packed = gather_layers(deep, jnp.zeros(TILE, jnp.float32))
         rhs_out[nt, j] = packed
         rhs_in[nt, j, 1, gy] = packed
         gathers = gather_copies(rhs_out.at[nt, j], rhs_in.at[nt, j], sb.at[nt, j], rb.at[nt, j])
@@ -374,33 +401,33 @@
         def up(i):
             mix = round_ext(nt, turn, i)
             for k, low in ((i, True), (i + half, False)):
-                def put():
+                def place_layer():
                     m = jnp.where(slot_e == k, around, 0.0)
-                    m = roll(m, lax.rem(LANES - (k & 3), LANES), 1)
+                    m = roll(m, -(k & 3), 1)
                     m = m + roll(m, 1, 1)
                     m = m + roll(m, 2, 1)
-                    m = roll(m, lax.rem(ROWS - (k >> 2), ROWS), 0)
+                    m = roll(m, -(k >> 2), 0)
                     m = m + roll(m, 1, 0)
                     m = m + roll(m, 2, 0)
                     both = spread_low(mix, 1, 1) if low else spread_high(mix, 1, 1)
-                    ya[k] = m + jnp.where(even_row, both, roll(both, 1, 0))
-                    b1[k] = jnp.where(even_row, roll(both, -1, 0), both)
-                put()
+                    put(ya, k, m + jnp.where(even_row, both, roll(both, 1, 0)))
+                    put(b1, k, jnp.where(even_row, roll(both, -1, 0), both))
+                place_layer()
         layers(up, half)
         sweep(lev1, ya, b1, yb, 2)
 
         def join(k):
-            field, left = residual(lev1, yb, b1, k, 2)
-            xb[k] = xb[k] + field + lev1[1, k] * left
+            field, left = residual(lev1, yb, b1, k, 2, 4, 16)
+            put(xb, k, get(xb, k, 4, 16) + field + get(lev1.at[1], k, 4, 16) * left, 4)
         layers(join)
-        sweep(lev0, xb, rhs, xa, 1)
-        sweep(lev0, xa, rhs, xb, 1)
+        sweep(lev0, xb, rhs, xa, 1, 4, 16)
+        sweep(lev0, xa, rhs, xb, 1, 4, 16)
         sent(gathers)
         sent(halo)
 
     def applied(k):
-        field = xb[k]
-        return (lev0[0, k] * field - pulled(lev0, xb, k, field, 1))[8:16, :128]
+        field = get(xb, k, 8, 8)
+        return (get(lev0.at[0], k, 8, 8) * field - pulled(lev0, xb, k, field, 1, 8, 8))[:, :128]
 
     def newton(nt, carry):
         def cells(k):
@@ -408,8 +435,8 @@
             saturation = res[k] + (1.0 - res[k]) * effective
             slope = (1.0 - res[k]) * alp[k] * effective * (1.0 - effective)
             rel[k] = effective * effective
-            xa[k] = STORAGE + por[k] * slope
-            g[k] = por[k] * (saturation - sat[k]) + STORAGE * (state[k] - old[k])
+            stored[k] = STORAGE + por[k] * slope
+            put(g, k, por[k] * (saturation - sat[k]) + STORAGE * (state[k] - old[k]))
         layers(cells)
 
         def faces(k):
@@ -419,41 +446,47 @@
                 return 2.0 * con[k] * con_n / jnp.where(live, total, 1.0) * (0.5 * (rel[k] + rel_n))
             west = face(roll(con[k], 1, 0), roll(rel[k], 1, 0))
             south = face(roll(con[k], 1, 1), roll(rel[k], 1, 1))
-            lower = face(con[jnp.maximum(k - 1, 0)], rel[jnp.maximum(k - 1, 0)])
-            lev0[2, k], lev0[3, k] = west, roll(west, -1, 0)
-            lev0[4, k], lev0[5, k] = south, roll(south, -1, 1)
-            lev0[6, k] = jnp.where(k > 0, lower, 0.0)
+            lower = face(con[k - 1], rel[k - 1]) if k else jnp.zeros((ROWS, LANES), jnp.float32)
+            for f, field in enumerate((west, roll(west, -1, 0), south, roll(south, -1, 1), lower)):
+                put(lev0.at[f + 2], k, field)
         layers(faces)
 
-        def operators(k, packed):
-            west, east, south, north, lower = (lev0[f, k] for f in range(2, 7))
-            upper = jnp.where(k < last, lev0[6, jnp.minimum(k + 1, last)], 0.0)
-            lev0[7, k] = upper
-            fine = (xa[k], west, east, south, north, lower, upper)
-            diag = fine[0] + west + east + south + north + lower + upper
-            lev0[0, k], lev0[1, k] = diag, OMEGA / diag
+        def operators(k, carried):
+            middle_lower, packed = carried
+            west, east, south, north, lower = (get(lev0.at[f], k) for f in range(2, 7))
+            upper = get(lev0.at[6], k + 1) if k < last else jnp.zeros((ROWS, LANES), jnp.float32)
+            put(lev0.at[7], k, upper)
+            diag = stored[k] + west + east + south + north + lower + upper
+            put(lev0.at[0], k, diag)
+            put(lev0.at[1], k, OMEGA / diag)
             here = state[k]
-            below, above = state[jnp.maximum(k - 1, 0)], state[jnp.minimum(k + 1, last)]
+            below, above = state[below_of(k)], state[above_of(k)]
             flux = (
                 west * (here - roll(here, 1, 0)) + east * (here - roll(here, -1, 0))
                 + south * (here - roll(here, 1, 1)) + north * (here - roll(here, -1, 1))
                 + lower * (here - below + 1.0) + upper * (here - above - 1.0)
             )
-            g[k] = jnp.where(k == last, rch[...], 0.0) - g[k] - flux
-            middle = coarsen(fine, 1)
+            gain = rch[...] - get(g, k) if k == last else -get(g, k)
+            put(g, k, gain - flux)
+            middle_west = spread_low(sum_pair(west, 1, 1), 1, 0)
+            middle_south = spread_low(sum_pair(south, 1, 0), 1, 1)
+            middle_upper = sum_four(upper, 1)
+            middle = (sum_four(stored[k], 1), middle_west, roll(middle_west, -2, 0), middle_south,
+                      roll(middle_south, -2, 1), middle_lower, middle_upper)
             diag = middle[0]
             for f in range(1, 7):
-                lev1[f + 1, k] = middle[f]
+                put(lev1.at[f + 1], k, middle[f])
                 diag = diag + middle[f]
-            lev1[0, k], lev1[1, k] = diag, OMEGA / diag
+            put(lev1.at[0], k, diag)
+            put(lev1.at[1], k, OMEGA / diag)
             coarse = coarsen([field[8:16, :128] for field in middle], 2)
             diag = coarse[0]
             for f in range(1, 7):
                 diag = diag + coarse[f]
             mixed = jnp.where((row8 & 4) == 0, coarse[2], sum_pair(coarse[0], 4, 0))
-            return tuple(jnp.where(slot8 == k, field, so_far)
-                         for field, so_far in zip((diag, coarse[3], coarse[5], mixed), packed))
-        packed = lax.fori_loop(0, depth, operators, (jnp.zeros(TILE, jnp.float32),) * 4, unroll=True)
+            return middle_upper, tuple(jnp.where(slot8 == k, field, so_far)
+                                       for field, so_far in zip((diag, coarse[3], coarse[5], mixed), packed))
+        _, packed = gather_layers(operators, (jnp.zeros((ROWS, LANES), jnp.float32), (jnp.zeros(TILE, jnp.float32),) * 4))
         for f in range(4):
             coarse_out[nt, f] = packed[f]
             coarse_in[nt, 1, gy, f] = packed[f]
@@ -465,16 +498,16 @@
 
         def image(k, sums):
             gg, gp, pp = sums
-            mine = g[k][8:16, :128]
+            mine = mine_of(g, k)
             diff = applied(k) - mine
-            z0[k] = xb[k][8:16, :128]
+            z0[k] = mine_of(xb, k)
             msg[nt, 3, k] = z0[k]
             put_edges(pack.at[nt, 3], k, z0[k])
             own[k] = diff
             msg[nt, 1, k] = diff
             put_edges(pack.at[nt, 1], k, diff)
             return gg + mine * mine, gp + mine * diff, pp + diff * diff
-        gg, gp, pp = lax.fori_loop(0, depth, image, (zeros, zeros, zeros), unroll=True)
+        gg, gp, pp = gather_layers(image, (zeros, zeros, zeros))
         halo = round_copies(nt, 1, depth)
         halo_z = round_copies(nt, 3, depth)
         halo_u = round_copies(nt, 4, depth)
@@ -486,20 +519,20 @@
             start(halo_z)
 
         def spread(k):
-            b0[k] = round_ext(nt, 1, k)
+            put(b0, k, round_ext(nt, 1, k))
         layers(spread)
         sent(halo)
         precondition(nt, 1, b0, None)
 
         def second(k, sums):
             gs, ps, ss = sums
-            mine = g[k][8:16, :128]
+            mine = mine_of(g, k)
             im = applied(k)
-            u = xb[k][8:16, :128]
+            u = mine_of(xb, k)
             msg[nt, 4, k] = u
             put_edges(pack.at[nt, 4], k, u)
             return gs + mine * im, ps + own[k] * im, ss + im * im
-        gs, ps, ss = lax.fori_loop(0, depth, second, (zeros, zeros, zeros), unroll=True)
+        gs, ps, ss = gather_layers(second, (zeros, zeros, zeros))
 
         rows = [jnp.sum(item, axis=0, keepdims=True) for item in (gg, gp, pp, gs, ps, ss)]
         tile = zeros
@@ -585,11 +618,12 @@
         return pltpu.SemaphoreType.DMA(shape)
 
     ext = vmem(depth, ROWS, LANES)
-    level = vmem(8, depth, ROWS, LANES)
+    flat = ROWS * depth + 16
+    level = vmem(8, 2, flat, 128)
     n0 = depth + 1
     assert n0 <= 16
-    scratch = [ext] * 7 + [vmem(ROWS, LANES), ext]
-    scratch += [level, level] + [ext] * 7 + [vmem(depth, *TILE)]
+    scratch = [ext] * 7 + [vmem(ROWS, LANES), ext, ext]
+    scratch += [level, level] + [vmem(2, flat, 128)] * 7 + [vmem(depth, *TILE)]
     scratch += [pltpu.VMEM((depth,) + TILE, jnp.int32)] + [pltpu.SMEM(item.shape, jnp.float32) for item in args[4:]]
     scratch += [
         vmem(depth, *TILE), vmem(3, n0, *TILE), vmem(3, n0, *TILE), vmem(3, n0, *TILE),
@@ -606,11 +640,11 @@
     return pl.pallas_call(
         functools.partial(kernel, gxn, gyn, depth),
         out_shape=jax.ShapeDtypeStruct(args[0].shape, jnp.float32),
-        in_specs=[pl.BlockSpec(memory_space=pl.ANY)] * 8,
+        in_specs=[pl.BlockSpec(memory_space=pltpu.HBM)] * 8,
         out_specs=pl.BlockSpec(memory_space=pltpu.VMEM),
         scratch_shapes=scratch,
         compiler_params=pltpu.CompilerParams(
-            collective_id=0, has_side_effects=True, vmem_limit_bytes=40 * 1024 * 1024),
+            collective_id=0, has_side_effects=True, vmem_limit_bytes=64 * 1024 * 1024),
     )(*args)
 
 

time: 85.6 us -> 79.4 us (0.928)
  local copies, waits for them, and re-layouts: 6.26 us -> 1.4 us
  Pallas kernels: 78.9 us -> 77.7 us
    unnamed x17 -> x1, local copies, waits for them, and re-layouts: 6.26 us -> 1.4 us
    pallas_call x1, Pallas kernels: 78.9 us -> 77.7 us  [on_device(): pl.pallas_call(functools.partial(kernel, gxn, gyn, depth), out_shape=jax....]
where the time goes in v4:
time: 79.4 us; the launch traced here: 79.2 us
  Pallas kernels  77.7 us (98%)
  local copies, waits for them, and re-layouts  1.4 us (2%)
    pallas_call x1, Pallas kernels, on_device(): pl.pallas_call(functools.partial(kernel, gxn, gyn, depth), out_shape=jax....  77.7 us

profile of v4, /device:TPU:0, one launch (start us, length us, event | category | flops | bytes accessed | tf_op | source)
XLA Modules:
  0.0 79.2 jit_solution(1005118537154906233)
XLA Ops:
  0.0 77.7 %shard_map.82 = f32[10,8,128]{2,1,0:T(8,128)} custom-call(f32[10,8,128]{2,1,0:T(8,128)} %pressure.1, f32[10,8,128]{2,1,0:T(8,128)} %saturation_old.1, s32[10,8,128]{2,1,0:T(8,128)} %soil_type.1, f32[8,128]{1,0:T(8,128)} %recharge.1, f32[24]{0:T(128)} %ksat_in.1, f32[24]{0:T(128)} %alpha_in.1, f32[24]{0:T(128)} %porosity_in.1, f32[24]{0:T(128)} %residual_in.1), custom_call_target="tpu_custom_call" | custom-call | tf_op jit(solution)/shard_map/pallas_call | solution.py:640
  77.8 1.4 %copy.10 = f32[10,8,128]{2,1,0:T(8,128)} copy(f32[10,8,128]{2,1,0:T(8,128)} %shard_map.82) | data formatting | bytes 81920

commit v5 on v4

--- a/solution.py
+++ b/solution.py
@@ -84,14 +84,10 @@
     has_s, has_n = gy > 0, gy < gyn - 1
     last = depth - 1
 
-    def inside(dx, dy):
-        x, y = gx + dx, gy + dy
-        return (x >= 0) & (x < gxn) & (y >= 0) & (y < gyn)
-
-    def place(dx, dy):
-        return (jnp.clip(gx + dx, 0, gxn - 1), jnp.clip(gy + dy, 0, gyn - 1))
-
-    assert depth % 2 == 0
+    def place(dx, j):
+        return (jnp.clip(gx + dx, 0, gxn - 1), lax.rem(gy + j, gyn))
+
+    assert depth % 2 == 0 and gyn > 2
     half = depth // 2
     fetches = [
         pltpu.make_async_copy(src, dst, local.at[i])
@@ -115,7 +111,7 @@
     for dx in (-1, 0, 1):
         for j in range(gyn):
             if (dx, j) != (0, 0):
-                @pl.when(inside(dx, 0))
+                @pl.when((gx + dx >= 0) & (gx + dx < gxn))
                 def _():
                     pl.semaphore_signal(barrier, inc=1, device_id=(jnp.clip(gx + dx, 0, gxn - 1), lax.rem(gy + j, gyn)), device_id_type=MESH)
     for j in range(1, gxn):
@@ -139,10 +135,12 @@
         packs[0, where] = jnp.where(group == at, moved, packs[0, where])
         packs[1, where] = jnp.where(group == ((at + 15) % 16), moved, packs[1, where])
 
-    def halo_copies(blocks, packs, to_w, to_e, to_n, to_s, send, recv):
+    def halo_copies(blocks, packs, to_w, to_e, to_n, to_s, send, recv, only_x=False):
         copies = []
         for d, (dx, dy) in enumerate(DIRECTIONS):
             rows = pl.ds(8 * (1 - dx), 8)
+            if only_x and dy != 0:
+                continue
             if dy == 0:
                 src, dst = blocks, (to_w if dx > 0 else to_e)
             elif dy > 0:
@@ -151,21 +149,27 @@
                 src, dst = packs.at[0], to_n.at[:, rows]
             copy = pltpu.make_async_remote_copy(
                 src_ref=src, dst_ref=dst, send_sem=send.at[d], recv_sem=recv.at[d],
-                device_id=place(dx, dy), device_id_type=MESH)
-            copies.append((copy, inside(dx, dy), inside(-dx, -dy)))
+                device_id=place(dx, dy % gyn), device_id_type=MESH)
+            copies.append((copy, dx))
         return copies
 
-    def gather_copies(src, dst, send, recv):
+    def gather_copies(src, dst, send, recv, tiles_for=None):
         copies = []
         for dx in (-1, 0, 1):
             for j in range(gyn):
                 if (dx, j) == (0, 0):
                     continue
+                tiles = pl.ds(*tiles_for(j)) if tiles_for else pl.ds(0, src.shape[0])
                 copy = pltpu.make_async_remote_copy(
-                    src_ref=src, dst_ref=dst.at[1 - dx, gy], send_sem=send.at[1 - dx, j], recv_sem=recv.at[1 - dx, j],
-                    device_id=(jnp.clip(gx + dx, 0, gxn - 1), lax.rem(gy + j, gyn)), device_id_type=MESH)
-                copies.append((copy, inside(dx, 0), inside(-dx, 0)))
+                    src_ref=src.at[tiles], dst_ref=dst.at[1 - dx, gy, tiles], send_sem=send.at[1 - dx, j],
+                    recv_sem=recv.at[1 - dx, j], device_id=place(dx, j), device_id_type=MESH)
+                copies.append((copy, dx))
         return copies
+
+    def right_side_tiles(j):
+        if j == 1:
+            return 1, 2
+        return (0, 2) if j == gyn - 1 else (1, 1)
 
     def sum_copies(src, dst, send, recv, count, along_x):
         copies = []
@@ -174,23 +178,28 @@
             copy = pltpu.make_async_remote_copy(
                 src_ref=src, dst_ref=dst.at[j], send_sem=send.at[j], recv_sem=recv.at[j],
                 device_id=to, device_id_type=MESH)
-            copies.append((copy, None, None))
+            copies.append((copy, 0))
         return copies
 
-    def each(copies, do, which):
-        for entry in copies:
-            if entry[which] is None:
-                do(entry[0])
+    def each(copies, do, sign):
+        for side, there in ((0, None), (-1, has_w), (1, has_e)):
+            group = [copy for copy, dx in copies if dx * sign == side]
+            if not group:
+                continue
+            if there is None:
+                for copy in group:
+                    do(copy)
             else:
-                @pl.when(entry[which])
+                @pl.when(there)
                 def _():
-                    do(entry[0])
+                    for copy in group:
+                        do(copy)
 
     def start(copies):
         each(copies, lambda copy: copy.start(), 1)
 
     def arrive(copies):
-        each(copies, lambda copy: copy.wait_recv(), 2)
+        each(copies, lambda copy: copy.wait_recv(), -1)
 
     def sent(copies):
         each(copies, lambda copy: copy.wait_send(), 1)
@@ -333,16 +342,21 @@
             msg[nt, turn, i] = mix
             put_edges(pack.at[nt, turn], i, mix)
         layers(stage_middle, half)
-        halo = round_copies(nt, turn, half)
+        rows = pl.ds(0, half)
+        halo = halo_copies(
+            msg.at[nt, turn, rows], pack.at[nt, turn], recv_w.at[nt, turn, rows], recv_e.at[nt, turn, rows],
+            recv_n.at[nt, turn], recv_s.at[nt, turn], sh.at[nt, turn], rh.at[nt, turn], True)
         start(halo)
 
         def deep(k, packed):
             _, left = residual(lev1, yb, b1, k, 2, 8, 8)
             return jnp.where(slot8 == k, sum_four(left[:, :128], 2), packed)
         packed = gather_layers(deep, jnp.zeros(TILE, jnp.float32))
-        rhs_out[nt, j] = packed
-        rhs_in[nt, j, 1, gy] = packed
-        gathers = gather_copies(rhs_out.at[nt, j], rhs_in.at[nt, j], sb.at[nt, j], rb.at[nt, j])
+        rhs_out[nt, j, 0] = pack[nt, turn, 0, 0]
+        rhs_out[nt, j, 1] = packed
+        rhs_out[nt, j, 2] = pack[nt, turn, 1, 0]
+        rhs_in[nt, j, 1, gy, 1] = packed
+        gathers = gather_copies(rhs_out.at[nt, j], rhs_in.at[nt, j], sb.at[nt, j], rb.at[nt, j], right_side_tiles)
         start(gathers)
 
         def strips_of(pick):
@@ -379,7 +393,7 @@
             strip[6], strip[7] = lower, over(lower)
             strip_sum[...] = strip_totals(jnp.where(first_row, 0.0, mixed))
         arrive(gathers)
-        b2 = strips_of(lambda s, y: rhs_in[nt, j, s, y])
+        b2 = strips_of(lambda s, y: rhs_in[nt, j, s, y, 1])
         below_sum = strip_sum[...]
         some = below_sum > 0.0
         mean = jnp.where(some, strip_totals(b2) / jnp.where(some, below_sum, 1.0), 0.0)
@@ -398,8 +412,12 @@
         slot_e = (row_e & 3) * 4 + (lane_e & 3)
         arrive(halo)
 
+        north, south = lax.rem(gy + 1, gyn), lax.rem(gy + gyn - 1, gyn)
+        from_n = [jnp.concatenate([rhs_in[nt, j, s, north, 0] for s in range(3)], axis=0)]
+        from_s = [jnp.concatenate([rhs_in[nt, j, s, south, 2] for s in range(3)], axis=0)]
+
         def up(i):
-            mix = round_ext(nt, turn, i)
+            mix = extended(i, msg[nt, turn, i], recv_w.at[nt, turn], recv_e.at[nt, turn], from_n, from_s)
             for k, low in ((i, True), (i + half, False)):
                 def place_layer():
                     m = jnp.where(slot_e == k, around, 0.0)
@@ -630,7 +648,7 @@
         vmem(3, 2, 1, *TILE), vmem(3, 1, ROWS, 128), vmem(3, 1, ROWS, 128),
         vmem(NEWTON, HALO, depth, *TILE), vmem(NEWTON, HALO, depth, *TILE), vmem(NEWTON, HALO, depth, *TILE),
         vmem(NEWTON, HALO, 2, 1, *TILE), vmem(NEWTON, HALO, 1, ROWS, 128), vmem(NEWTON, HALO, 1, ROWS, 128),
-        vmem(NEWTON, 4, *TILE), vmem(NEWTON, 3, gyn, 4, *TILE), vmem(NEWTON, 2, *TILE), vmem(NEWTON, 2, 3, gyn, *TILE),
+        vmem(NEWTON, 4, *TILE), vmem(NEWTON, 3, gyn, 4, *TILE), vmem(NEWTON, 2, 3, *TILE), vmem(NEWTON, 2, 3, gyn, 3, *TILE),
         vmem(8, ROWS, 128 * gyn), vmem(ROWS, 128), vmem(gyn, ROWS, 128),
         vmem(NEWTON, *TILE), vmem(NEWTON, gyn, *TILE), vmem(NEWTON, gxn, *TILE), vmem(NEWTON, *TILE),
         dma(8), dma(3, 8), dma(3, 8), dma(NEWTON, HALO, 8), dma(NEWTON, HALO, 8),

time: 79.4 us -> 80.3 us (1.011)
  Pallas kernels: 77.7 us -> 78.6 us
    pallas_call x1, Pallas kernels: 77.7 us -> 78.6 us  [on_device(): pl.pallas_call(functools.partial(kernel, gxn, gyn, depth), out_shape=jax....]
where the time goes in v5:
time: 80.3 us; the launch traced here: 80 us
  Pallas kernels  78.6 us (98%)
  local copies, waits for them, and re-layouts  1.4 us (2%)
    pallas_call x1, Pallas kernels, on_device(): pl.pallas_call(functools.partial(kernel, gxn, gyn, depth), out_shape=jax....  78.6 us

profile of v5, /device:TPU:0, one launch (start us, length us, event | category | flops | bytes accessed | tf_op | source)
XLA Modules:
  0.0 80.0 jit_solution(4718674313652401310)
XLA Ops:
  0.0 78.6 %shard_map.82 = f32[10,8,128]{2,1,0:T(8,128)} custom-call(f32[10,8,128]{2,1,0:T(8,128)} %pressure.1, f32[10,8,128]{2,1,0:T(8,128)} %saturation_old.1, s32[10,8,128]{2,1,0:T(8,128)} %soil_type.1, f32[8,128]{1,0:T(8,128)} %recharge.1, f32[24]{0:T(128)} %ksat_in.1, f32[24]{0:T(128)} %alpha_in.1, f32[24]{0:T(128)} %porosity_in.1, f32[24]{0:T(128)} %residual_in.1), custom_call_target="tpu_custom_call" | custom-call | tf_op jit(solution)/shard_map/pallas_call | solution.py:658
  78.6 1.4 %copy.10 = f32[10,8,128]{2,1,0:T(8,128)} copy(f32[10,8,128]{2,1,0:T(8,128)} %shard_map.82) | data formatting | bytes 81920

commit v6 on v4

--- a/solution.py
+++ b/solution.py
@@ -76,8 +76,8 @@
     own, msg0, recv0_w, recv0_e, pack0, recv0_n, recv0_s,
     msg, recv_w, recv_e, pack, recv_n, recv_s,
     coarse_out, coarse_in, rhs_out, rhs_in, strip, strip_sum, solved,
-    part_out, part_y, part_x, whole_x,
-    local, s0, r0, sh, rh, sc, rc, sb, rb, sy, ry, sx, rx,
+    part_out, part_in,
+    local, s0, r0, sh, rh, sc, rc, sb, rb, sx, rx,
 ):
     gx, gy = lax.axis_index("gx"), lax.axis_index("gy")
     has_w, has_e = gx > 0, gx < gxn - 1
@@ -112,18 +112,13 @@
         ref[...] = jnp.zeros(ref.shape, ref.dtype)
 
     barrier = pltpu.get_barrier_semaphore()
-    for dx in (-1, 0, 1):
-        for j in range(gyn):
-            if (dx, j) != (0, 0):
-                @pl.when(inside(dx, 0))
-                def _():
-                    pl.semaphore_signal(barrier, inc=1, device_id=(jnp.clip(gx + dx, 0, gxn - 1), lax.rem(gy + j, gyn)), device_id_type=MESH)
-    for j in range(1, gxn):
-        x = lax.rem(gx + j, gxn)
-        @pl.when((x != gx - 1) & (x != gx + 1))
-        def _():
-            pl.semaphore_signal(barrier, inc=1, device_id=(x, gy), device_id_type=MESH)
-    strips = 1 + has_w.astype(jnp.int32) + has_e.astype(jnp.int32)
+    others = [(i, j) for i in range(gxn) for j in range(gyn) if (i, j) != (0, 0)]
+
+    def around_by(i, j):
+        return (lax.rem(gx + i, gxn), lax.rem(gy + j, gyn))
+
+    for i, j in others:
+        pl.semaphore_signal(barrier, inc=1, device_id=around_by(i, j), device_id_type=MESH)
 
     lane8, row8 = iota(TILE, 1), iota(TILE, 0)
     slot8 = (row8 & 3) * 4 + (lane8 & 3)
@@ -167,13 +162,12 @@
                 copies.append((copy, inside(dx, 0), inside(-dx, 0)))
         return copies
 
-    def sum_copies(src, dst, send, recv, count, along_x):
+    def sum_copies(src, dst, send, recv):
         copies = []
-        for j in range(1, count):
-            to = (lax.rem(gx + j, gxn), gy) if along_x else (gx, lax.rem(gy + j, gyn))
+        for i, j in others:
             copy = pltpu.make_async_remote_copy(
-                src_ref=src, dst_ref=dst.at[j], send_sem=send.at[j], recv_sem=recv.at[j],
-                device_id=to, device_id_type=MESH)
+                src_ref=src, dst_ref=dst.at[i * gyn + j], send_sem=send.at[i, j], recv_sem=recv.at[i, j],
+                device_id=around_by(i, j), device_id_type=MESH)
             copies.append((copy, None, None))
         return copies
 
@@ -248,7 +242,7 @@
         fetch.wait()
     layers(lambda k: put_edges(pack0.at[1], k, msg0[1, k]))
     layers(lambda k: put_edges(pack0.at[2], k, msg0[2, k]), depth + 1)
-    pl.semaphore_wait(barrier, gyn * strips - 1 + gxn - strips)
+    pl.semaphore_wait(barrier, len(others))
     groups = [first_copies(0, depth), first_copies(1, depth), first_copies(2, depth + 1)]
     for group in groups:
         start(group)
@@ -534,26 +528,25 @@
             return gs + mine * im, ps + own[k] * im, ss + im * im
         gs, ps, ss = gather_layers(second, (zeros, zeros, zeros))
 
-        rows = [jnp.sum(item, axis=0, keepdims=True) for item in (gg, gp, pp, gs, ps, ss)]
         tile = zeros
-        for i, item in enumerate(rows):
-            tile = jnp.where(row8 == i, jnp.broadcast_to(item, TILE), tile)
-        part_out[nt] = tile
-        along_y = sum_copies(part_out.at[nt], part_y.at[nt], sy.at[nt], ry.at[nt], gyn, False)
-        start(along_y)
+        for i, item in enumerate((gg, gp, pp, gs, ps, ss)):
+            tile = jnp.where(row8 == i, jnp.broadcast_to(jnp.sum(item, axis=0, keepdims=True), TILE), tile)
+        for step in (64, 32, 16):
+            tile = tile + roll(tile, step, 1)
+        own_lanes = (lane8 >> 4) == row8
+        part_out[nt] = jnp.sum(jnp.where(own_lanes, tile, 0.0), axis=0, keepdims=True)
+        part_in[nt, 0] = part_out[nt]
+        sums = sum_copies(part_out.at[nt], part_in.at[nt], sx.at[nt], rx.at[nt])
+        start(sums)
 
         @pl.when(nt < NEWTON - 1)
         def _():
             start(halo_u)
-        arrive(along_y)
-        for j in range(1, gyn):
-            tile = tile + part_y[nt, j]
-        whole_x[nt] = tile
-        along_x = sum_copies(whole_x.at[nt], part_x.at[nt], sx.at[nt], rx.at[nt], gxn, True)
-        start(along_x)
-        arrive(along_x)
-        for j in range(1, gxn):
-            tile = tile + part_x[nt, j]
+        arrive(sums)
+        whole = part_in[nt, 0]
+        for i in range(1, gxn * gyn):
+            whole = whole + part_in[nt, i]
+        tile = jnp.where(own_lanes, jnp.broadcast_to(whole, TILE), 0.0)
         totals = jnp.broadcast_to(jnp.sum(tile, axis=1, keepdims=True), (8, LANES))
         gg, gp, pp, gs, ps, ss = (totals[i:i + 1] for i in range(6))
 
@@ -601,8 +594,7 @@
                           + second_weight[:, :128] * msg[nt, 4, k])
             layers(finish)
         sent(operator)
-        sent(along_y)
-        sent(along_x)
+        sent(sums)
         return carry
 
     lax.fori_loop(0, NEWTON, newton, 0)
@@ -632,10 +624,10 @@
         vmem(NEWTON, HALO, 2, 1, *TILE), vmem(NEWTON, HALO, 1, ROWS, 128), vmem(NEWTON, HALO, 1, ROWS, 128),
         vmem(NEWTON, 4, *TILE), vmem(NEWTON, 3, gyn, 4, *TILE), vmem(NEWTON, 2, *TILE), vmem(NEWTON, 2, 3, gyn, *TILE),
         vmem(8, ROWS, 128 * gyn), vmem(ROWS, 128), vmem(gyn, ROWS, 128),
-        vmem(NEWTON, *TILE), vmem(NEWTON, gyn, *TILE), vmem(NEWTON, gxn, *TILE), vmem(NEWTON, *TILE),
+        vmem(NEWTON, 1, 128), vmem(NEWTON, gxn * gyn, 1, 128),
         dma(8), dma(3, 8), dma(3, 8), dma(NEWTON, HALO, 8), dma(NEWTON, HALO, 8),
         dma(NEWTON, 3, gyn), dma(NEWTON, 3, gyn), dma(NEWTON, 2, 3, gyn), dma(NEWTON, 2, 3, gyn),
-        dma(NEWTON, gyn), dma(NEWTON, gyn), dma(NEWTON, gxn), dma(NEWTON, gxn),
+        dma(NEWTON, gxn, gyn), dma(NEWTON, gxn, gyn),
     ]
     return pl.pallas_call(
         functools.partial(kernel, gxn, gyn, depth),

time: 79.4 us -> 78.1 us (0.984)
  Pallas kernels: 77.7 us -> 76.4 us
    pallas_call x1, Pallas kernels: 77.7 us -> 76.4 us  [on_device(): pl.pallas_call(functools.partial(kernel, gxn, gyn, depth), out_shape=jax....]
where the time goes in v6:
time: 78.1 us; the launch traced here: 77.8 us
  Pallas kernels  76.4 us (98%)
  local copies, waits for them, and re-layouts  1.4 us (2%)
    pallas_call x1, Pallas kernels, on_device(): pl.pallas_call(functools.partial(kernel, gxn, gyn, depth), out_shape=jax....  76.4 us

profile of v6, /device:TPU:0, one launch (start us, length us, event | category | flops | bytes accessed | tf_op | source)
XLA Modules:
  0.0 77.8 jit_solution(15011526516424613203)
XLA Ops:
  0.0 76.4 %shard_map.82 = f32[10,8,128]{2,1,0:T(8,128)} custom-call(f32[10,8,128]{2,1,0:T(8,128)} %pressure.1, f32[10,8,128]{2,1,0:T(8,128)} %saturation_old.1, s32[10,8,128]{2,1,0:T(8,128)} %soil_type.1, f32[8,128]{1,0:T(8,128)} %recharge.1, f32[24]{0:T(128)} %ksat_in.1, f32[24]{0:T(128)} %alpha_in.1, f32[24]{0:T(128)} %porosity_in.1, f32[24]{0:T(128)} %residual_in.1), custom_call_target="tpu_custom_call" | custom-call | tf_op jit(solution)/shard_map/pallas_call | solution.py:632
  76.4 1.4 %copy.10 = f32[10,8,128]{2,1,0:T(8,128)} copy(f32[10,8,128]{2,1,0:T(8,128)} %shard_map.82) | data formatting | bytes 81920
